TPU v7x, 512 devices: a whole 4x8x8 slice. The times are simulated.
512 devices in a mesh: grp: 8 (over y), ep: 64 (over x, z, core).
Axes of the slice: x: 4, y: 8, z: 8, core: 2. Of those that a mesh axis runs over, the one named last changes fastest.
Arguments:
- hidden_in: bfloat16 [4096, 2048], P('ep'), may hold values from -45 to 45
- query_nope: bfloat16 [4096, 2048], P('ep', 'grp'), may hold values from -6 to 6
- query_rope: bfloat16 [4096, 1024], P('ep', 'grp'), may hold values from -56 to 56
- new_latent: bfloat16 [1024, 2304], P('ep'), may hold values from -6 to 6
- latent_cache: bfloat16 [4096, 9216], P('ep'), may hold values from -6 to 6
- key_absorb: bfloat16 [16, 128, 512], P('grp'), may hold values from -0.5 to 0.5
- value_absorb: bfloat16 [16, 512, 128], P('grp'), may hold values from -1 to 1
- output_proj: bfloat16 [2048, 2048], P('grp'), may hold values from -0.125 to 0.125
- norm_gain: bfloat16 [2048], replicated, may hold values from 0.099609375 to 1.8984375
- router_proj: bfloat16 [2048, 64], replicated, may hold values from -0.125 to 0.125
- expert_ids: int32 [4096, 6], P('ep'), may hold values from 0 to 63, all different within a row; in each aligned block of 64 rows (0 to 63, 64 to 127, ...) at most 8 rows name the same one
- expert_gate: bfloat16 [64, 2048, 1408], P('ep', None, 'grp'), may hold values from -0.125 to 0.125
- expert_up: bfloat16 [64, 2048, 1408], P('ep', None, 'grp'), may hold values from -0.125 to 0.125
- expert_down: bfloat16 [64, 1408, 2048], P('ep', 'grp'), may hold values from -0.15625 to 0.15625
- block_table: int32 [1024, 64], P('ep'), may hold values from 0 to 191, as said below
- lengths: int32 [1024], P('ep'), may hold values from 1 to 1024
- subtree_moves: int32 [64, 64, 2], P('ep'), may hold values from -1 to 63, as said below
Outputs:
- mixed: bfloat16 [4096, 2048], P('ep', 'grp')
Inputs may be any that keep to these rules, and one draw needn't show every extreme that they name: `expert_ids`: within the rows of one ep index no expert is named by more than 8 entries, a bound that some block reaches. `subtree_moves`: never the source itself; a live entry is a block id of the source; for every destination the rank after it sends 2 live blocks. `block_table`: an address names a resident block or a live moved block of that request's rank; the addresses of one request are distinct; the requests of a rank share a leading run of moved blocks.
All inputs are finite; a program needn't handle non-finite values.
Results may differ from a plain program's by a relative error of at most 0.0074.
Values may be sent and summed in bfloat16 or wider, within the bound.
A program may use at most 64 MiB of HBM per device.

v0:
```python
import jax
import jax.numpy as jnp
from jax import lax
from jax.sharding import PartitionSpec as P


def local(
    hidden_in,
    query_nope,
    query_rope,
    new_latent,
    latent_cache,
    key_absorb,
    value_absorb,
    output_proj,
    norm_gain,
    router_proj,
    expert_ids,
    expert_gate,
    expert_up,
    expert_down,
    block_table,
    lengths,
    subtree_moves,
):
    head_count = key_absorb.shape[0]
    nope_dim = key_absorb.shape[1]
    latent_dim = key_absorb.shape[2]
    rope_dim = query_rope.shape[1] // head_count
    key_width = latent_dim + rope_dim
    requests, table_len = block_table.shape
    step_count = new_latent.shape[1] // key_width
    row_count = hidden_in.shape[0]
    model_dim = hidden_in.shape[1]
    block_size = latent_cache.shape[1] // key_width
    cached = table_len * block_size
    scale_of_scores = (nope_dim + rope_dim) ** (-0.5)
    local_blocks = latent_cache.shape[0]
    group_size = lax.axis_size("grp")
    group_index = lax.axis_index("grp")
    sent_ids = subtree_moves[0]
    picked_blocks = latent_cache[jnp.clip(sent_ids, 0, local_blocks - 1)]
    outgoing = jnp.where((sent_ids >= 0)[:, :, None], picked_blocks, jnp.zeros_like(picked_blocks))
    arrived = lax.all_to_all(outgoing, "ep", split_axis=0, concat_axis=0, tiled=True)
    block_pool = jnp.concatenate([latent_cache, arrived.reshape(-1, latent_cache.shape[1])], axis=0)
    q_latent = jnp.einsum(
        "rhc,hcl->rhl",
        query_nope.reshape(row_count, head_count, nope_dim),
        key_absorb,
        preferred_element_type=jnp.float32,
    ).astype(jnp.bfloat16)
    queries = jnp.concatenate(
        [q_latent, query_rope.reshape(row_count, head_count, rope_dim)], axis=2
    ).reshape(requests, step_count * head_count, key_width)
    fresh_keys = new_latent.reshape(requests, step_count, key_width)
    per_step = 2
    key_pos = jnp.arange(cached + step_count, dtype=jnp.int32)
    row_step = jnp.arange(step_count * head_count, dtype=jnp.int32) // head_count

    def attend(request_group):
        start_row = request_group * per_step
        table_rows = lax.dynamic_slice_in_dim(block_table, start_row, per_step, 0)
        key_rows = block_pool[table_rows].reshape(per_step, cached, key_width)
        key_rows = jnp.concatenate(
            [key_rows, lax.dynamic_slice_in_dim(fresh_keys, start_row, per_step, 0)], axis=1
        )
        query_rows = lax.dynamic_slice_in_dim(queries, start_row, per_step, 0)
        limits = lax.dynamic_slice_in_dim(lengths, start_row, per_step, 0)
        score_values = (
            jnp.einsum("gqw,gkw->gqk", query_rows, key_rows, preferred_element_type=jnp.float32)
            * scale_of_scores
        )
        visible = jnp.where(
            key_pos[None, None, :] < cached,
            key_pos[None, None, :] < limits[:, None, None],
            key_pos[None, None, :] - cached <= row_step[None, :, None],
        )
        score_values = jnp.where(visible, score_values, -1e30)
        row_peak = jnp.max(score_values, axis=2, keepdims=True)
        exp_scores = jnp.exp(score_values - row_peak)
        attention = (exp_scores / jnp.sum(exp_scores, axis=2, keepdims=True)).astype(jnp.bfloat16)
        return jnp.einsum(
            "gqk,gkl->gql",
            attention,
            key_rows[:, :, :latent_dim],
            preferred_element_type=jnp.float32,
        ).astype(jnp.bfloat16)

    latent_out = lax.map(attend, jnp.arange(requests // per_step, dtype=jnp.int32)).reshape(
        row_count, head_count, latent_dim
    )
    head_out = (
        jnp.einsum("rhl,hlv->rhv", latent_out, value_absorb, preferred_element_type=jnp.float32)
        .astype(jnp.bfloat16)
        .reshape(row_count, -1)
    )
    partial_value = jnp.dot(head_out, output_proj, preferred_element_type=jnp.float32)
    attention_out = lax.psum(partial_value, "grp")
    residual_state = hidden_in.astype(jnp.float32) + attention_out
    normed = (
        residual_state
        * lax.rsqrt(jnp.mean(residual_state * residual_state, axis=1, keepdims=True) + 1e-06)
        * norm_gain.astype(jnp.float32)
    ).astype(jnp.bfloat16)
    logits = jnp.dot(normed, router_proj, preferred_element_type=jnp.float32)
    chosen = jax.nn.sigmoid(jnp.take_along_axis(logits, expert_ids, axis=1))
    gate_weights = chosen / jnp.sum(chosen, axis=1, keepdims=True)
    experts = router_proj.shape[1]
    top_count = expert_ids.shape[1]
    per_device = expert_gate.shape[0]
    capacity = max(2, (4 * row_count * top_count + 3 * experts - 1) // (3 * experts))
    flat_ids = expert_ids.reshape(-1)
    onehot = (flat_ids[:, None] == jnp.arange(experts, dtype=jnp.int32)[None, :]).astype(jnp.int32)
    slot_index = jnp.sum((jnp.cumsum(onehot, axis=0) - 1) * onehot, axis=1)
    target = (flat_ids * capacity + slot_index).reshape(row_count, top_count)
    selector = jnp.any(
        target[None, :, :] == jnp.arange(experts * capacity, dtype=jnp.int32)[:, None, None], axis=2
    ).astype(jnp.bfloat16)
    buffer = (
        jnp.dot(selector, normed, preferred_element_type=jnp.float32)
        .astype(jnp.bfloat16)
        .reshape(experts // per_device, per_device, capacity, model_dim)
    )
    width_out = model_dim // group_size
    column_index = group_index * width_out
    expert_rows = lax.all_to_all(buffer, "ep", split_axis=0, concat_axis=0, tiled=True)
    gate_proj = jnp.einsum(
        "sekd,edf->sekf", expert_rows, expert_gate, preferred_element_type=jnp.float32
    )
    up_proj = jnp.einsum(
        "sekd,edf->sekf", expert_rows, expert_up, preferred_element_type=jnp.float32
    )
    activated = (jax.nn.silu(gate_proj) * up_proj).astype(jnp.bfloat16)
    results = jnp.einsum(
        "sekf,efd->sekd", activated, expert_down, preferred_element_type=jnp.float32
    )
    returned = lax.all_to_all(
        results.astype(jnp.bfloat16), "ep", split_axis=0, concat_axis=0, tiled=True
    ).astype(results.dtype)
    gathered = returned.reshape(experts * capacity, -1)[target]
    expert_mix = lax.psum_scatter(
        jnp.sum(gate_weights[:, :, None] * gathered, axis=1).astype(jnp.bfloat16),
        "grp",
        scatter_dimension=1,
        tiled=True,
    ).astype(jnp.float32)
    state_part = lax.dynamic_slice_in_dim(residual_state, column_index, width_out, 1)
    return (state_part + expert_mix).astype(jnp.bfloat16)


def solution(mesh):
    in_specs = (
        P("ep", None),
        P("ep", "grp"),
        P("ep", "grp"),
        P("ep", None),
        P("ep", None),
        P("grp", None, None),
        P("grp", None, None),
        P("grp", None),
        P(),
        P(),
        P("ep", None),
        P("ep", None, "grp"),
        P("ep", None, "grp"),
        P("ep", "grp", None),
        P("ep", None),
        P("ep"),
        P("ep", None, None),
    )
    out_specs = P("ep", "grp")
    return jax.shard_map(local, mesh=mesh, in_specs=in_specs, out_specs=out_specs, check_vma=False)
```

profile of v0, /device:TPU:1, one launch (start us, length us, event | category | flops | bytes accessed | tf_op | source)
XLA Modules:
  0.0 508.9 jit_solution(12526684080895337938)
XLA Ops:
  8.2 7.0 %gather_fusion.1 = bf16[128,9216]{1,0:T(8,128)(2,1)} fusion(bf16[64,9216]{1,0:T(8,128)(2,1)} %param.23, s32[1024]{0:T(1024)S(1)} %pad_clamp_fusion.2), kind=kCustom, calls=%fused_computation.1 | custom fusion | bytes 4719104 | tf_op jit(solution)/shard_map/gather | solution.py:42
  18.2 3.5 broadcast_select_fusion
  21.7 15.1 %all-to-all-start = ((bf16[64,2,9216]{2,1,0:T(2,128)(2,1)}), bf16[64,2,9216]{2,1,0:T(2,128)(2,1)}, u32[]{:S(2)}, u32[]{:S(2)}) async-start(bf16[64,2,9216]{2,1,0:T(2,128)(2,1)} %broadcast_select_fusion), calls=%async_computation | async-start | bytes 4718592 | tf_op jit(solution)/shard_map/all_to_all | solution.py:44
  40.4 53.1 %all-to-all-done = bf16[64,2,9216]{2,1,0:T(2,128)(2,1)} async-done(((bf16[64,2,9216]{2,1,0:T(2,128)(2,1)}), bf16[64,2,9216]{2,1,0:T(2,128)(2,1)}, u32[]{:S(2)}, u32[]{:S(2)}) %all-to-all-start) | async-done | bytes 2359328 | tf_op jit(solution)/shard_map/all_to_all | solution.py:44
  93.4 4.3 reshape.220
  97.7 3.7 pad_maximum_fusion
  101.4 146.3 %while.14 = (s32[]{:T(128)}, bf16[8,2,8,512]{3,2,1,0:T(8,128)(2,1)}, s32[8]{0:T(128)S(1)}, s32[16]{0:T(128)S(1)}, bf16[16,8,576]{2,1,0:T(8,128)(2,1)}, /*index=5...) while((s32[]{:T(128)}, ...), condition=%wide.region_3.4_spmd.clone.clone, body=%wide.region_0.3_spmd.clone.clone.sunk | while | flops 44876728 | bytes 14924303 | solution.py:89
  103.3 6.6 %gather_fusion = bf16[128,9216]{1,0:T(8,128)(2,1)S(1)} fusion(bf16[192,9216]{1,0:T(8,128)(2,1)} %get-tuple-element.286, s32[1024]{0:T(1024)S(1)} %pad_clamp_fusion.4), kind=kCustom, calls=%fused_computation.clone.clone.1 | custom fusion | bytes 4719104 | tf_op jit(solution)/shard_map/while/body/eval_jaxpr/gather | solution.py:63
  121.6 6.6 %gather_fusion = bf16[128,9216]{1,0:T(8,128)(2,1)S(1)} fusion(bf16[192,9216]{1,0:T(8,128)(2,1)} %get-tuple-element.286, s32[1024]{0:T(1024)S(1)} %pad_clamp_fusion.4), kind=kCustom, calls=%fused_computation.clone.clone.1 | custom fusion | bytes 4719104 | tf_op jit(solution)/shard_map/while/body/eval_jaxpr/gather | solution.py:63
  139.9 6.6 %gather_fusion = bf16[128,9216]{1,0:T(8,128)(2,1)S(1)} fusion(bf16[192,9216]{1,0:T(8,128)(2,1)} %get-tuple-element.286, s32[1024]{0:T(1024)S(1)} %pad_clamp_fusion.4), kind=kCustom, calls=%fused_computation.clone.clone.1 | custom fusion | bytes 4719104 | tf_op jit(solution)/shard_map/while/body/eval_jaxpr/gather | solution.py:63
  158.2 6.6 %gather_fusion = bf16[128,9216]{1,0:T(8,128)(2,1)S(1)} fusion(bf16[192,9216]{1,0:T(8,128)(2,1)} %get-tuple-element.286, s32[1024]{0:T(1024)S(1)} %pad_clamp_fusion.4), kind=kCustom, calls=%fused_computation.clone.clone.1 | custom fusion | bytes 4719104 | tf_op jit(solution)/shard_map/while/body/eval_jaxpr/gather | solution.py:63
  176.5 6.6 %gather_fusion = bf16[128,9216]{1,0:T(8,128)(2,1)S(1)} fusion(bf16[192,9216]{1,0:T(8,128)(2,1)} %get-tuple-element.286, s32[1024]{0:T(1024)S(1)} %pad_clamp_fusion.4), kind=kCustom, calls=%fused_computation.clone.clone.1 | custom fusion | bytes 4719104 | tf_op jit(solution)/shard_map/while/body/eval_jaxpr/gather | solution.py:63
  194.7 6.6 %gather_fusion = bf16[128,9216]{1,0:T(8,128)(2,1)S(1)} fusion(bf16[192,9216]{1,0:T(8,128)(2,1)} %get-tuple-element.286, s32[1024]{0:T(1024)S(1)} %pad_clamp_fusion.4), kind=kCustom, calls=%fused_computation.clone.clone.1 | custom fusion | bytes 4719104 | tf_op jit(solution)/shard_map/while/body/eval_jaxpr/gather | solution.py:63
  213.0 6.6 %gather_fusion = bf16[128,9216]{1,0:T(8,128)(2,1)S(1)} fusion(bf16[192,9216]{1,0:T(8,128)(2,1)} %get-tuple-element.286, s32[1024]{0:T(1024)S(1)} %pad_clamp_fusion.4), kind=kCustom, calls=%fused_computation.clone.clone.1 | custom fusion | bytes 4719104 | tf_op jit(solution)/shard_map/while/body/eval_jaxpr/gather | solution.py:63
  231.3 6.6 %gather_fusion = bf16[128,9216]{1,0:T(8,128)(2,1)S(1)} fusion(bf16[192,9216]{1,0:T(8,128)(2,1)} %get-tuple-element.286, s32[1024]{0:T(1024)S(1)} %pad_clamp_fusion.4), kind=kCustom, calls=%fused_computation.clone.clone.1 | custom fusion | bytes 4719104 | tf_op jit(solution)/shard_map/while/body/eval_jaxpr/gather | solution.py:63
  251.8 69.8 %all-reduce.2.cloned.1.call-done = f32[64,2048]{1,0:T(8,128)} async-done(((f32[64,2048]{1,0:T(8,128)}), f32[64,2048]{1,0:T(8,128)}) %all-reduce.2.cloned.1.call-update) | async-done | bytes 524304 | tf_op jit(solution)/shard_map/psum | solution.py:98
  323.6 67.0 %all_to_all.15 = bf16[64,1,8,2048]{3,2,1,0:T(8,128)(2,1)S(1)} all-to-all(bf16[64,1,8,2048]{3,2,1,0:T(8,128)(2,1)S(1)} %fusion.51), channel_id=1, replica_groups=mesh['grp'=8,'ep'=64] {'ep'}, dimensions={0} | all-to-all | bytes 4194304 | tf_op jit(solution)/shard_map/all_to_all | solution.py:126
  392.2 5.1 %fusion.50 = bf16[64,1,8,2048]{3,2,1,0:T(8,128)(2,1)} fusion(bf16[1,176,2048]{2,1,0:T(8,128)(2,1)} %param.32, bf16[64,1,8,2048]{3,2,1,0:T(8,128)(2,1)S(1)} %all_to_all.15, bf16[1,2048,176]{1,2,0:T(8,128)(2,1)} %param.31, f32[64,1,8,176]{3,2,0,1:T(8,128)} %fusion.56), kind=kOutput, calls=%fused_computation.49 | convolution fusion | flops 739786752 | bytes 5996544 | tf_op jit(solution)/shard_map/sekf,efd->sekd/dot_general | solution.py:134
  397.3 5.9 %all-to-all-start.2 = ((bf16[64,1,8,2048]{3,2,1,0:T(8,128)(2,1)}), bf16[64,1,8,2048]{3,2,1,0:T(8,128)(2,1)S(1)}, u32[]{:S(2)}, u32[]{:S(2)}) async-start(bf16[64,1,8,2048]{3,2,1,0:T(8,128)(2,1)} %fusion.50), calls=%async_computation.2 | async-start | bytes 4194304 | tf_op jit(solution)/shard_map/all_to_all | solution.py:137
  408.4 46.1 %all-to-all-done.2 = bf16[64,1,8,2048]{3,2,1,0:T(8,128)(2,1)S(1)} async-done(((bf16[64,1,8,2048]{3,2,1,0:T(8,128)(2,1)}), bf16[64,1,8,2048]{3,2,1,0:T(8,128)(2,1)S(1)}, u32[]{:S(2)}, u32[]{:S(2)}) %all-to-all-start.2) | async-done | bytes 2097184 | tf_op jit(solution)/shard_map/all_to_all | solution.py:137
  457.0 7.3 %gather_fusion.2 = f32[384,2048]{1,0:T(8,128)} fusion(f32[512,2048]{1,0:T(8,128)} %bitcast_convert_fusion, s32[1024]{0:T(1024)S(1)} %pad_clamp_fusion.1), kind=kCustom, calls=%fused_computation.2 | custom fusion | bytes 6292992 | tf_op jit(solution)/shard_map/gather | solution.py:140
  464.3 4.6 reshape.254
  468.8 4.5 multiply_reduce_fusion
  473.3 27.2 %reduce-scatter.2.cloned.1.call-done = bf16[64,256]{1,0:T(8,128)(2,1)} async-done(((bf16[64,2048]{1,0:T(8,128)(2,1)}), bf16[64,256]{1,0:T(8,128)(2,1)}) %reduce-scatter.2.cloned.1.call-update) | async-done | bytes 32784 | tf_op jit(solution)/shard_map/reduce_scatter | solution.py:141
  (192 shorter events, 113.3 us)
Async XLA Ops:
  6.5 243.3 %copy-start = (bf16[256,2048]{1,0:T(8,128)(2,1)S(1)}, bf16[256,2048]{1,0:T(8,128)(2,1)}, u32[]{:S(2)}) copy-start(bf16[256,2048]{1,0:T(8,128)(2,1)} %param.26) | copy-start | bytes 3145732
  21.7 15.4 %copy-start.6 = (s32[64,6]{0,1:T(8,128)S(1)}, s32[64,6]{0,1:T(8,128)}, u32[]{:S(2)}) copy-start(s32[64,6]{0,1:T(8,128)} %param.29) | copy-start | bytes 4612
  21.7 16.7 %copy-start.4 = (bf16[2,128,512]{2,1,0:T(8,128)(2,1)S(1)}, bf16[2,128,512]{2,1,0:T(8,128)(2,1)}, u32[]{:S(2)}) copy-start(bf16[2,128,512]{2,1,0:T(8,128)(2,1)} %param.24) | copy-start | bytes 786436
  21.7 16.7 %copy-start.8 = (bf16[64,256]{1,0:T(8,128)(2,1)S(1)}, bf16[64,256]{1,0:T(8,128)(2,1)}, u32[]{:S(2)}) copy-start(bf16[64,256]{1,0:T(8,128)(2,1)} %param.20) | copy-start | bytes 98308
  21.7 17.1 %copy-start.9 = (bf16[64,128]{1,0:T(8,128)(2,1)S(1)}, bf16[64,128]{1,0:T(8,128)(2,1)}, u32[]{:S(2)}) copy-start(bf16[64,128]{1,0:T(8,128)(2,1)} %param.21) | copy-start | bytes 49156
  21.7 17.2 %copy-start.7 = (bf16[16,2304]{1,0:T(8,128)(2,1)S(1)}, bf16[16,2304]{1,0:T(8,128)(2,1)}, u32[]{:S(2)}) copy-start(bf16[16,2304]{1,0:T(8,128)(2,1)} %param.22) | copy-start | bytes 221188
  21.7 71.7 %all-to-all-start = ((bf16[64,2,9216]{2,1,0:T(2,128)(2,1)}), bf16[64,2,9216]{2,1,0:T(2,128)(2,1)}, u32[]{:S(2)}, u32[]{:S(2)}) async-start(bf16[64,2,9216]{2,1,0:T(2,128)(2,1)} %broadcast_select_fusion), calls=%async_computation | async-start | bytes 4718592 | tf_op jit(solution)/shard_map/all_to_all | solution.py:44
  36.9 284.7 %all-reduce.2.cloned.1.call-start = ((), (), s32[]{:S(2)}) async-start(), calls=%async_computation.4 | async-start | bytes 1048576 | tf_op jit(solution)/shard_map/psum | solution.py:98
  40.4 57.4 %copy-start.1 = (bf16[64,9216]{1,0:T(8,128)(2,1)S(1)}, bf16[64,9216]{1,0:T(8,128)(2,1)}, u32[]{:S(2)}) copy-start(bf16[64,9216]{1,0:T(8,128)(2,1)} %param.23) | copy-start | bytes 3538948
  97.7 3.7 copy-start.12
  247.7 3.9 copy-start.10
  247.7 73.9 %copy-start.3 = (bf16[64,2048]{1,0:T(8,128)(2,1)S(1)}, bf16[64,2048]{1,0:T(8,128)(2,1)}, u32[]{:S(2)}) copy-start(bf16[64,2048]{1,0:T(8,128)(2,1)} %param.19) | copy-start | bytes 786436
  322.8 67.8 %copy-start.2 = (f32[64,2048]{1,0:T(8,128)}, f32[64,2048]{1,0:T(8,128)S(1)}, u32[]{:S(2)}) copy-start(f32[64,2048]{1,0:T(8,128)S(1)} %get-tuple-element.200) | copy-start | bytes 1572868
  323.6 67.0 %copy-start.11 = (bf16[1,2048,176]{1,2,0:T(8,128)(2,1)S(1)}, bf16[1,2048,176]{1,2,0:T(8,128)(2,1)}, u32[]{:S(2)}) copy-start(bf16[1,2048,176]{1,2,0:T(8,128)(2,1)} %param.30) | copy-start | bytes 2162692
  397.3 6.5 %copy-start.5 = (bf16[2048,64]{0,1:T(8,128)(2,1)S(1)}, bf16[2048,64]{0,1:T(8,128)(2,1)}, u32[]{:S(2)}) copy-start(bf16[2048,64]{0,1:T(8,128)(2,1)} %param.28) | copy-start | bytes 786436
  397.3 57.2 %all-to-all-start.2 = ((bf16[64,1,8,2048]{3,2,1,0:T(8,128)(2,1)}), bf16[64,1,8,2048]{3,2,1,0:T(8,128)(2,1)S(1)}, u32[]{:S(2)}, u32[]{:S(2)}) async-start(bf16[64,1,8,2048]{3,2,1,0:T(8,128)(2,1)} %fusion.50), calls=%async_computation.2 | async-start | bytes 4194304 | tf_op jit(solution)/shard_map/all_to_all | solution.py:137
  403.3 97.3 %reduce-scatter.2.cloned.1.call-start = ((), (), s32[]{:S(2)}) async-start(), calls=%async_computation.5 | async-start | bytes 294912 | tf_op jit(solution)/shard_map/reduce_scatter | solution.py:141
Sparse Core Ops, SparseCore 0:
  251.1 70.4 all-reduce.1
  473.5 27.0 reduce-scatter.1
where the time goes:
time: 516 us; the launch traced here: 509 us
  waiting for transfers between devices  196 us (38%)
  local copies, waits for them, and re-layouts  124 us (24%)
  blocking collectives  67 us (13%)
  matrix products  54.4 us (11%)
  other arithmetic  27.2 us (5%)
  starting transfers between devices  21.4 us (4%)
  between operations  13.7 us (3%)
    psum x1, waiting for transfers between devices, local(): attention_out = lax.psum(partial_value, 'grp')  69.8 us
    all_to_all x1, blocking collectives, local(): lax.all_to_all(buffer, 'ep', split_axis=0, concat_axis=0, tiled=True)  67 us
    all_to_all x1, waiting for transfers between devices, local(): lax.all_to_all(outgoing, 'ep', split_axis=0, concat_axis=0, tiled=True)  53.1 us
    gather x8, local copies, waits for them, and re-layouts, attend(): key_rows = block_pool[table_rows].reshape(per_step, cached, key_width)  52.9 us
    all_to_all x1, waiting for transfers between devices, local(): lax.all_to_all(results.astype(jnp.bfloat16), 'ep', split_axis=0, concat_a...  46.1 us
    reduce_scatter x1, waiting for transfers between devices, local(): lax.psum_scatter(jnp.sum(gate_weights[:, :, None] * gathered, axis=1).ast...  27.2 us
    reshape x8, local copies, waits for them, and re-layouts, attend(): key_rows = block_pool[table_rows].reshape(per_step, cached, key_width)  26.9 us
    sub x8, matrix products, attend(): exp_scores = jnp.exp(score_values - row_peak)  21.9 us
  transfers between devices with their start and end apart: 4, of which 4 were waited for; matrix products, arithmetic and copies ran while one was open for 2% of the time, Pallas kernels for 0%

commit v1 on v0

v1 whole, which is shorter than its diff:
```python
import jax
import jax.numpy as jnp
from jax import lax
from jax.experimental import pallas as pl
from jax.experimental.pallas import tpu as pltpu
from jax.sharding import PartitionSpec as P

BF = jnp.bfloat16
F32 = jnp.float32
MESH = pl.DeviceIdType.MESH
NG = 8
NE = 64
NEG = -1e30


def iota(shape, dim):
    return lax.broadcasted_iota(jnp.int32, shape, dim)


def hot(condition):
    return jnp.where(condition, 1.0, 0.0).astype(BF)


def dot(a, b):
    return jnp.dot(a, b, preferred_element_type=F32)


def dot_nt(a, b):
    return lax.dot_general(a, b, (((1,), (1,)), ((), ())), preferred_element_type=F32)


def dot_tn(a, b):
    return lax.dot_general(a, b, (((0,), (0,)), ((), ())), preferred_element_type=F32)


def await_bytes(ref, sem):
    pltpu.make_async_copy(ref, ref, sem).wait()


def kernel(
    len_ref, hid, qn, qr, nl, ka, va, op, gain, router, ids, bt, mv, cache_hbm, wg_hbm, wu_hbm, wd_hbm,
    out,
    cache, wg, wu, wd, msg, pool, qe, qo, acc_e, acc_o, p3s, p3r, p4s, p4r, lgs, lgr, st, xs, gath,
    acc_g, acc_u, act, part, rsr, ys, ret,
    cache_sem, w_sem, e1s, e1r, a1s, a1r, p3ss, p3rs, p4ss, p4rs, lgss, lgrs, e2s, e2r, a2s, a2r, rss, rsrs, e3s, e3r,
):
    g = lax.axis_index("grp")
    me = lax.axis_index("ep")
    scale = (128 + 64) ** (-0.5)

    def peer(k):
        return lax.rem(g + (k + NG), NG)

    barrier = pltpu.get_barrier_semaphore()

    def greet(k, carry):
        pl.semaphore_signal(barrier, inc=1, device_id={"ep": lax.rem(me + k, NE)}, device_id_type=MESH)
        return carry

    lax.fori_loop(1, NE, greet, 0)
    for k in range(1, NG):
        pl.semaphore_signal(barrier, inc=1, device_id={"grp": peer(k)}, device_id_type=MESH)

    for p in range(8):
        pltpu.make_async_copy(cache_hbm.at[:, pl.ds(1152 * p, 1152)], cache.at[p], cache_sem).start()
    w_copies = [
        pltpu.make_async_copy(wg_hbm.at[0], wg, w_sem.at[0]),
        pltpu.make_async_copy(wu_hbm.at[0], wu, w_sem.at[1]),
        pltpu.make_async_copy(wd_hbm.at[0], wd, w_sem.at[2]),
    ]
    for copy in w_copies:
        copy.start()

    lo_me = lax.rem(me, 8)
    lo_to = lax.rem(g - lo_me + 8, 8)
    row = iota((128, 64), 0)
    sel = hot(iota((128, 64), 1) == lo_to + 8 * (row // 16))
    picked = dot(sel, mv[0].astype(F32).astype(BF))
    rk = iota((128, 1), 0)
    blk = jnp.where((rk // 8) % 2 == 0, picked[:, 0:1], picked[:, 1:2])
    code = jnp.where(blk < -0.5, -1.0, blk + (64 * (rk % 8)).astype(F32)).astype(jnp.int32)
    big = hot(iota((128, 512), 1) == code)
    await_bytes(cache, cache_sem)
    msg[...] = dot(big, cache[...].reshape(512, 1152)).astype(BF).reshape(8, 16, 1152)

    pl.semaphore_wait(barrier, NE - 1 + NG - 1)

    mine = me // 8
    for j in range(8):
        to = lo_to + 8 * j

        @pl.when(to == me)
        def _():
            pltpu.make_async_copy(msg.at[j], pool.at[g, mine], e1r.at[mine // 4]).start()

        @pl.when(to != me)
        def _():
            pltpu.make_async_remote_copy(
                msg.at[j], pool.at[g, mine], e1s, e1r.at[mine // 4], device_id={"ep": to}, device_id_type=MESH
            ).start()

    for h in range(2):
        rows = pl.ds(64 * h, 64)
        q_lat = dot(qn[:, 128 * h : 128 * h + 128], ka[h]).astype(BF)
        a, b = iota((128, 128), 0), iota((128, 128), 1)
        rope = dot(qr[...], hot((b < 64) & (a == b + 64 * h))).astype(BF)
        qe[rows, 0:512] = q_lat
        qe[rows, 512:640] = rope
    qo[...] = dot(qe[...], hot(iota((640, 640), 1) == iota((640, 640), 0) + 64)).astype(BF)

    req = iota((16, 64), 0)
    lens = jnp.zeros((16, 64), jnp.int32)
    for i in range(16):
        lens = jnp.where(req == i, len_ref[i], lens)
    count = jnp.clip(lens - 16 * iota((16, 64), 1), 0, 16)
    table = bt[...]
    addr = iota((16, 192), 1)
    usable = jnp.zeros((16, 192), jnp.int32)
    for p in range(64):
        usable = usable + jnp.where(table[:, p : p + 1] == addr, count[:, p : p + 1], 0)
    lam = iota((128, 16), 0)
    spread = hot((lam % 64) // 4 == iota((128, 16), 1))
    usable = dot(spread, usable.astype(F32).astype(BF)).astype(BF)

    acc_e[...] = jnp.zeros_like(acc_e)
    acc_o[...] = jnp.zeros_like(acc_o)

    def attend(x, c, m, l):
        even, odd = c > 0.5, c > 1.5
        s_e = jnp.where(even, dot_nt(qe[...], x[:, 0:640]) * scale, NEG)
        s_o = jnp.where(odd, dot_nt(qo[...], x[:, 512:1152]) * scale, NEG)
        peak = jnp.maximum(jnp.max(s_e, axis=1, keepdims=True), jnp.max(s_o, axis=1, keepdims=True))
        m_new = jnp.maximum(m, peak)
        p_e = jnp.where(even, jnp.exp(s_e - m_new), 0.0)
        p_o = jnp.where(odd, jnp.exp(s_o - m_new), 0.0)
        f = jnp.exp(m - m_new)
        l = l * f + jnp.sum(p_e, axis=1, keepdims=True) + jnp.sum(p_o, axis=1, keepdims=True)
        acc_e[...] = acc_e[...] * f + dot(p_e.astype(BF), x[:, 0:512])
        acc_o[...] = acc_o[...] * f + dot(p_o.astype(BF), x[:, 512:1152])
        return m_new, l

    stats = (jnp.full((128, 1), NEG, F32), jnp.zeros((128, 1), F32))
    lam, key = iota((128, 32), 0), iota((128, 32), 1)
    c_new = jnp.where((lam % 64) // 4 == key % 16, lam % 4 + 1 - 2 * (key // 16), 0).astype(F32)
    fresh = jnp.concatenate([nl[:, 0:1152], nl[:, 1152:2304]], axis=0)
    stats = attend(fresh, c_new, *stats)
    c_res = dot(usable, hot(iota((192, 128), 0) == iota((192, 128), 1) % 64))
    half_of = (iota((128, 128), 1) // 64).astype(F32)
    for q in range(4):
        x = cache[pl.ds(2 * q, 2)].reshape(128, 1152)
        stats = attend(x, c_res - 2.0 * (2 * q + half_of), *stats)

    def ring_gather(at, ssem, rsem, ready, on_chunk):
        def send(o, h, way):
            pltpu.make_async_remote_copy(
                at(o, h), at(o, h), ssem, rsem.at[h, o], device_id={"grp": peer(way)}, device_id_type=MESH
            ).start()

        def got(o, h):
            await_bytes(at(o, h), rsem.at[h, o])

        for h in range(2):
            ready(h)
            send(g, h, 1)
            send(g, h, -1)
        on_chunk(g)
        for t in range(3):
            a, b = peer(-1 - t), peer(1 + t)
            got(a, 0)
            send(a, 0, 1)
            got(b, 1)
            send(b, 1, -1)
            got(a, 1)
            if t < 2:
                send(a, 1, 1)
            got(b, 0)
            if t < 2:
                send(b, 0, -1)
            on_chunk(a)
            on_chunk(b)
        last = peer(4)
        got(last, 0)
        got(last, 1)
        on_chunk(last)

    carried = [stats]
    pair = ((iota((128, 128), 1) % 8) * 2).astype(F32)

    def attend_origin(o):
        col = iota((192, 128), 1)
        source = lax.rem(o - lo_me + 8, 8) + 8 * (col // 16)
        place = hot(iota((192, 128), 0) == 64 + 2 * source + (col // 8) % 2)
        c = dot(usable, place) - pair
        carried[0] = attend(pool[o].reshape(128, 1152), c, *carried[0])

    ring_gather(
        lambda o, h: pool.at[o, pl.ds(4 * h, 4)],
        a1s,
        a1r,
        lambda h: await_bytes(pool.at[g, pl.ds(4 * h, 4)], e1r.at[h]),
        attend_origin,
    )
    total = acc_e[...] + acc_o[...][:, 64:576]
    latent = (total / carried[0][1]).astype(BF)
    heads = [dot(latent[64 * h : 64 * h + 64], va[h]).astype(BF) for h in range(2)]
    term = dot(heads[0], op[0:128]) + dot(heads[1], op[128:256])
    for c in range(8):
        p3s[c] = term[:, 256 * c : 256 * c + 256].astype(BF)

    def exchange(src, dst, ssem, rsem):
        for k in range(1, NG):
            pltpu.make_async_remote_copy(
                src(peer(k)), dst.at[k - 1], ssem, rsem, device_id={"grp": peer(k)}, device_id_type=MESH
            ).start()

    exchange(lambda c: p3s.at[c], p3r, p3ss, p3rs)
    ids_v = ids[...]
    lane_e = iota((64, 64), 1)
    named = jnp.zeros((64, 64), F32)
    for k in range(6):
        named = named + jnp.where(ids_v[:, k : k + 1] == lane_e, 1.0, 0.0)
    named_b = named.astype(BF)
    before = dot(hot(iota((64, 64), 1) < iota((64, 64), 0)), named_b).astype(BF)
    widen = hot(iota((64, 512), 1) // 8 == iota((64, 512), 0))
    slot = (iota((64, 512), 1) % 8).astype(F32)
    chosen = (dot(named_b, widen) > 0.5) & (jnp.abs(dot(before, widen) - slot) < 0.5)
    chosen_b = hot(chosen)

    await_bytes(p3r, p3rs)
    cols = pl.ds(pl.multiple_of(g * 256, 256), 256)
    attn = p3s[g].astype(F32)
    for k in range(NG - 1):
        attn = attn + p3r[k].astype(F32)
    state = hid[:, cols].astype(F32) + attn
    st[...] = state
    square = jnp.sum(state * state, axis=1, keepdims=True)
    diagonal = iota((64, 128), 0) == iota((64, 128), 1)
    p4s[...] = jnp.broadcast_to(jnp.sum(jnp.where(diagonal, square, 0.0), axis=0, keepdims=True), (8, 128))
    exchange(lambda c: p4s, p4r, p4ss, p4rs)
    await_bytes(p4r, p4rs)
    squares = p4s[...]
    for k in range(NG - 1):
        squares = squares + p4r[k]
    square = jnp.sum(jnp.where(diagonal, squares[0:1], 0.0), axis=1, keepdims=True)
    inverse = lax.rsqrt(square / 2048.0 + 1e-06)
    normed = (state * inverse * gain[:, cols].astype(F32)).astype(BF)

    xs[...] = dot_tn(chosen_b, normed).reshape(64, 8, 256).astype(BF)
    pltpu.make_async_copy(xs.at[me], gath.at[g, me], e2r.at[me // 32]).start()

    def dispatch(k, carry):
        to = lax.rem(me + k, NE)
        pltpu.make_async_remote_copy(
            xs.at[to], gath.at[g, me], e2s, e2r.at[me // 32], device_id={"ep": to}, device_id_type=MESH
        ).start()
        return carry

    lax.fori_loop(1, NE, dispatch, 0)
    lgs[...] = dot(normed, router[pl.ds(pl.multiple_of(g * 256, 256), 256), :])
    exchange(lambda c: lgs, lgr, lgss, lgrs)
    for copy in w_copies:
        copy.wait()
    acc_g[...] = jnp.zeros_like(acc_g)
    acc_u[...] = jnp.zeros_like(acc_u)

    def expert_columns(o):
        x = gath[o].reshape(512, 256)
        rows = pl.ds(pl.multiple_of(o * 256, 256), 256)
        acc_g[...] += dot(x, wg[rows, :])
        acc_u[...] += dot(x, wu[rows, :])

    ring_gather(
        lambda o, h: gath.at[o, pl.ds(32 * h, 32)],
        a2s,
        a2r,
        lambda h: await_bytes(gath.at[g, pl.ds(32 * h, 32)], e2r.at[h]),
        expert_columns,
    )
    gate = acc_g[...]
    act[...] = (gate / (1.0 + jnp.exp(-gate)) * acc_u[...]).astype(BF)

    def make(c):
        lanes = pl.ds(pl.multiple_of(c * 256, 256), 256)
        part[c] = dot(act[...], wd[:, lanes]).reshape(64, 8, 256).astype(BF)

    def half(h):
        return pl.ds(32 * h, 32)

    def pass_on(c, h, way):
        d = 0 if way > 0 else 1
        pltpu.make_async_remote_copy(
            part.at[c, half(h)], rsr.at[d, c, half(h)], rss, rsrs.at[d, h, c],
            device_id={"grp": peer(way)}, device_id_type=MESH,
        ).start()

    def add_in(c, h, way):
        d = 0 if way > 0 else 1
        await_bytes(rsr.at[d, c, half(h)], rsrs.at[d, h, c])
        part[c, half(h)] = (part[c, half(h)].astype(F32) + rsr[d, c, half(h)].astype(F32)).astype(BF)

    make(peer(4))
    pass_on(peer(4), 0, 1)
    pass_on(peer(4), 1, -1)
    make(peer(3))
    pass_on(peer(3), 1, 1)
    make(peer(-3))
    pass_on(peer(-3), 0, -1)
    for t in range(1, 4):
        if t < 3:
            make(peer(3 - t))
            make(peer(t - 3))
        else:
            make(g)
        add_in(peer(4 - t), 0, 1)
        pass_on(peer(4 - t), 0, 1)
        add_in(peer(t - 4), 1, -1)
        pass_on(peer(t - 4), 1, -1)
        if t < 3:
            add_in(peer(3 - t), 1, 1)
            pass_on(peer(3 - t), 1, 1)
            add_in(peer(t - 3), 0, -1)
            pass_on(peer(t - 3), 0, -1)

    for h in range(2):
        total_h = part[g, half(h)].astype(F32)
        for d in range(2):
            await_bytes(rsr.at[d, g, half(h)], rsrs.at[d, h, g])
            total_h = total_h + rsr[d, g, half(h)].astype(F32)
        ys[half(h)] = total_h.astype(BF)

    pltpu.make_async_copy(ys.at[me], ret.at[me], e3r).start()

    def give_back(k, carry):
        to = lax.rem(me + k, NE)
        pltpu.make_async_remote_copy(
            ys.at[to], ret.at[me], e3s, e3r, device_id={"ep": to}, device_id_type=MESH
        ).start()
        return carry

    lax.fori_loop(1, NE, give_back, 0)

    await_bytes(lgr, lgrs)
    logits = lgs[...]
    for k in range(NG - 1):
        logits = logits + lgr[k]
    weight = jnp.where(named > 0.5, jax.nn.sigmoid(logits), 0.0)
    weight = weight / jnp.sum(weight, axis=1, keepdims=True)
    w_hi = weight.astype(BF)
    w_lo = (weight - w_hi.astype(F32)).astype(BF)
    mask = chosen_b.astype(F32)
    mix_hi = (dot(w_hi, widen) * mask).astype(BF)
    mix_lo = (dot(w_lo, widen) * mask).astype(BF)
    await_bytes(ret, e3r)
    results = ret[...].reshape(512, 256)
    out[...] = (st[...] + dot(mix_hi, results) + dot(mix_lo, results)).astype(BF)

    @pl.when(lax.rem(2 * me, 8) == g)
    def _():
        await_bytes(msg.at[pl.ds(0, 7)], e1s)

    @pl.when(lax.rem(2 * me, 8) != g)
    def _():
        await_bytes(msg, e1s)

    await_bytes(pool.at[pl.ds(0, 7)], a1s)
    await_bytes(p3s.at[pl.ds(0, 7)], p3ss)
    await_bytes(p4r, p4ss)
    await_bytes(lgr, lgss)
    await_bytes(xs.at[pl.ds(0, 63)], e2s)
    await_bytes(gath.at[pl.ds(0, 7)], a2s)
    await_bytes(part.at[pl.ds(0, 7)], rss)
    await_bytes(ys.at[pl.ds(0, 63)], e3s)


def local(
    hidden_in, query_nope, query_rope, new_latent, latent_cache, key_absorb, value_absorb, output_proj, norm_gain,
    router_proj, expert_ids, expert_gate, expert_up, expert_down, block_table, lengths, subtree_moves,
):
    vmem = pl.BlockSpec(memory_space=pltpu.VMEM)
    anywhere = pl.BlockSpec(memory_space=pl.ANY)
    dma = pltpu.SemaphoreType.DMA
    v = pltpu.VMEM
    return pl.pallas_call(
        kernel,
        out_shape=jax.ShapeDtypeStruct((64, 256), BF),
        in_specs=[pl.BlockSpec(memory_space=pltpu.SMEM)] + [vmem] * 12 + [anywhere] * 4,
        out_specs=vmem,
        scratch_shapes=[
            v((8, 64, 1152), BF),
            v((2048, 176), BF),
            v((2048, 176), BF),
            v((176, 2048), BF),
            v((8, 16, 1152), BF),
            v((8, 8, 16, 1152), BF),
            v((128, 640), BF),
            v((128, 640), BF),
            v((128, 512), F32),
            v((128, 640), F32),
            v((8, 64, 256), BF),
            v((7, 64, 256), BF),
            v((8, 128), F32),
            v((7, 8, 128), F32),
            v((64, 64), F32),
            v((7, 64, 64), F32),
            v((64, 256), F32),
            v((64, 8, 256), BF),
            v((8, 64, 8, 256), BF),
            v((512, 176), F32),
            v((512, 176), F32),
            v((512, 176), BF),
            v((8, 64, 8, 256), BF),
            v((2, 8, 64, 8, 256), BF),
            v((64, 8, 256), BF),
            v((64, 8, 256), BF),
            dma, dma((3,)),
            dma, dma((2,)), dma, dma((2, 8)),
            dma, dma, dma, dma, dma, dma,
            dma, dma((2,)), dma, dma((2, 8)),
            dma, dma((2, 2, 8)),
            dma, dma,
        ],
        compiler_params=pltpu.CompilerParams(
            collective_id=0, has_side_effects=True, vmem_limit_bytes=56 * 1024 * 1024
        ),
        name="layer",
    )(
        lengths, hidden_in, query_nope, query_rope, new_latent, key_absorb, value_absorb, output_proj,
        norm_gain.reshape(1, -1), router_proj, expert_ids, block_table, subtree_moves,
        latent_cache, expert_gate, expert_up, expert_down,
    )


def solution(mesh):
    in_specs = (
        P("ep", None), P("ep", "grp"), P("ep", "grp"), P("ep", None), P("ep", None),
        P("grp", None, None), P("grp", None, None), P("grp", None), P(), P(), P("ep", None),
        P("ep", None, "grp"), P("ep", None, "grp"), P("ep", "grp", None), P("ep", None), P("ep"),
        P("ep", None, None),
    )
    return jax.shard_map(local, mesh=mesh, in_specs=in_specs, out_specs=P("ep", "grp"), check_vma=False)
```

time: 516 us -> 141 us (0.27); the launches traced: 509 us -> 141 us
  waiting for transfers between devices: 196 us -> 0 us
  Pallas kernels: 0 us -> 131 us
  local copies, waits for them, and re-layouts: 124 us -> 10.1 us
  blocking collectives: 67 us -> 0 us
  matrix products: 54.4 us -> 0 us
  other arithmetic: 27.2 us -> 0 us
  starting transfers between devices: 21.4 us -> 0 us
  between operations: 13.7 us -> 0.01 us
    pallas_call x0 -> x1, Pallas kernels: none -> 131 us  [local(): pl.pallas_call(kernel, out_shape=jax.ShapeDtypeStruct((64, 256), BF), in_...]
    all_to_all x2 -> x0, waiting for transfers between devices: 99.2 us -> none  [the longest x1 53.1 us: local(): lax.all_to_all(outgoing, 'ep', split_axis=0, concat_axis=0, tiled=True)]
    gather x17 -> x0, local copies, waits for them, and re-layouts: 77.9 us -> none  [the longest x8 52.9 us: attend(): key_rows = block_pool[table_rows].reshape(per_step, cached, key_width)]
    psum x1 -> x0, waiting for transfers between devices: 69.8 us -> none  [local(): attention_out = lax.psum(partial_value, 'grp')]
    all_to_all x1 -> x0, blocking collectives: 67 us -> none  [local(): lax.all_to_all(buffer, 'ep', split_axis=0, concat_axis=0, tiled=True)]
    dot_general x15 -> x0, matrix products: 32.5 us -> none  [the longest x8 21.3 us: attend(): jnp.einsum('gqk,gkl->gql', attention, key_rows[:, :, :latent_dim], prefer...]
    reshape x11 -> x1, local copies, waits for them, and re-layouts: 32.9 us -> 1.37 us  [local(): norm_gain.reshape(1, -1)]
    reduce_scatter x1 -> x0, waiting for transfers between devices: 27.2 us -> none  [local(): lax.psum_scatter(jnp.sum(gate_weights[:, :, None] * gathered, axis=1).ast...]
  transfers between devices with their start and end apart: 4 -> 0, of which waited for: 4 -> 0; matrix products, arithmetic and copies ran while one was open for 2% -> 0% of each run, Pallas kernels for 0% -> 0%
where the time goes in v1:
time: 141 us
  Pallas kernels  131 us (93%)
  local copies, waits for them, and re-layouts  10.1 us (7%)
    pallas_call x1, Pallas kernels, local(): pl.pallas_call(kernel, out_shape=jax.ShapeDtypeStruct((64, 256), BF), in_...  131 us
    unnamed x10, local copies, waits for them, and re-layouts  8.73 us

profile of v1, /device:TPU:1, one launch (start us, length us, event | category | flops | bytes accessed | tf_op | source)
XLA Modules:
  0.0 140.9 jit_solution(8271402907095210548)
XLA Ops:
  0.0 0.0 copy-start
  0.0 1.4 reshape.3.gain
  1.4 1.4 copy.19.ids
  2.8 1.4 copy.20.mv
  4.1 0.0 copy-start.1
  4.1 2.0 %copy.18.router = bf16[2048,64]{1,0:T(8,128)(2,1)} copy(bf16[2048,64]{0,1:T(8,128)(2,1)} %param.26) | data formatting | bytes 524288 | tf_op args[9]
  6.1 0.0 copy-done
  6.2 1.3 copy.21.wg_hbm
  7.4 0.0 copy-done.1
  7.4 1.3 copy.22.wu_hbm
  8.7 130.7 %layer.1 = bf16[64,256]{1,0:T(8,128)(2,1)} custom-call(s32[16]{0:T(128)} %len_ref.1, bf16[64,2048]{1,0:T(8,128)(2,1)} %hid.1, bf16[64,256]{1,0:T(8,128)(2,1)} %qn.1, bf16[64,128]{1,0:T(8,128)(2,1)} %qr.1, bf16[16,2304]{1,0:T(8,128)(2,1)} %nl.1, bf16[2,128,512]{2,1,0:T(8,128)(2,1)} %ka.1, bf16[2,512,128]{2,1,0:T(8,128)(2,1)} %va.1, bf16[256,2048]{1,0:T(8,128)(2,1)} %op.1, ...), custom_call_target="tpu_custom_call" | custom-call | tf_op jit(solution)/shard_map/layer/pallas_call | solution.py:383
  139.5 1.4 copy.24
Async XLA Ops:
  0.0 6.2 %copy-start = (bf16[1,2048,176]{1,2,0:T(8,128)(2,1)S(1)}, bf16[1,2048,176]{1,2,0:T(8,128)(2,1)}, u32[]{:S(2)}) copy-start(bf16[1,2048,176]{1,2,0:T(8,128)(2,1)} %param.28) | copy-start | bytes 2162692
  4.1 3.3 %copy-start.1 = (bf16[1,2048,176]{1,2,0:T(8,128)(2,1)S(1)}, bf16[1,2048,176]{1,2,0:T(8,128)(2,1)}, u32[]{:S(2)}) copy-start(bf16[1,2048,176]{1,2,0:T(8,128)(2,1)} %param.29) | copy-start | bytes 2162692

commit v2 on v1

v2 whole, which is shorter than its diff:
```python
import jax
import jax.numpy as jnp
from jax import lax
from jax.experimental import pallas as pl
from jax.experimental.pallas import tpu as pltpu
from jax.sharding import PartitionSpec as P

BF = jnp.bfloat16
F32 = jnp.float32
MESH = pl.DeviceIdType.MESH
NG = 8
NE = 64
NEG = -1e30


def iota(shape, dim):
    return lax.broadcasted_iota(jnp.int32, shape, dim)


def hot(condition):
    return jnp.where(condition, 1.0, 0.0).astype(BF)


def dot(a, b):
    return jnp.dot(a, b, preferred_element_type=F32)


def dot_nt(a, b):
    return lax.dot_general(a, b, (((1,), (1,)), ((), ())), preferred_element_type=F32)


def dot_tn(a, b):
    return lax.dot_general(a, b, (((0,), (0,)), ((), ())), preferred_element_type=F32)


def await_bytes(ref, sem):
    pltpu.make_async_copy(ref, ref, sem).wait()


def kernel(
    len_ref, hid, qn, qr, nl, ka, va, op, gain, router, ids, bt, mv, cache_hbm, wg_hbm, wu_hbm, wd_hbm,
    out,
    wg, wu, wd, msg, far, pool, qe, qo, use, m_ref, l_ref, acc_e, acc_o, p3s, p3r, p4s, p4r, lgs, lgr, st, xs, gath,
    acc_g, acc_u, act, part, rsr, ys, ret,
    cache_sem, w_sem, e1s, e1r, n1s, n1r, a1s, a1r, p3ss, p3rs, p4ss, p4rs, lgss, lgrs, e2s, e2r, a2s, a2r, rss, rsrs, e3s, e3r,
):
    g = lax.axis_index("grp")
    me = lax.axis_index("ep")
    scale = (128 + 64) ** (-0.5)
    sent = []

    def peer(k):
        return lax.rem(g + (k + NG), NG)

    def loop(lo, hi, body):
        def step(i, carry):
            body(i)
            return carry

        lax.fori_loop(lo, hi, step, 0)

    barrier = pltpu.get_barrier_semaphore()
    loop(1, NE, lambda k: pl.semaphore_signal(
        barrier, inc=1, device_id={"ep": lax.rem(me + k, NE)}, device_id_type=MESH))
    loop(1, NG, lambda k: pl.semaphore_signal(barrier, inc=1, device_id={"grp": peer(k)}, device_id_type=MESH))

    cache = pool.at[pl.ds(3, 4)]
    for p in range(8):
        pltpu.make_async_copy(
            cache_hbm.at[:, pl.ds(1152 * p, 1152)], pool.at[3 + p // 2, pl.ds(64 * (p % 2), 64)], cache_sem
        ).start()
    w_copies = [
        pltpu.make_async_copy(wg_hbm, wg, w_sem.at[0]),
        pltpu.make_async_copy(wu_hbm, wu, w_sem.at[1]),
        pltpu.make_async_copy(wd_hbm.at[0], wd, w_sem.at[2]),
    ]
    for copy in w_copies:
        copy.start()

    z = (me // 2) % 8
    xc = (me // 16) * 2 + me % 2

    def rank(xc_, z_):
        return (xc_ // 2) * 16 + z_ * 2 + xc_ % 2

    await_bytes(cache, cache_sem)

    def build(k):
        row = iota((128, 64), 0)
        slot_ = row // 16
        to_far = jnp.where(slot_ < 5, rank(lax.rem(g - xc + 8, 8), lax.rem(z + 2 + slot_, 8)), -1)
        to_near = rank(slot_, lax.rem(z + k + 7, 8))
        sel = hot(iota((128, 64), 1) == jnp.where(k == 3, to_far, to_near))
        picked = dot_nt(sel, mv[...].astype(F32).astype(BF))
        rk = iota((128, 1), 0)
        blk = jnp.where((rk // 8) % 2 == 0, picked[:, 0:1], picked[:, 1:2])
        code = jnp.where(blk < -0.5, -1.0, blk + (64 * (rk % 8)).astype(F32)).astype(jnp.int32)
        big = hot(iota((128, 512), 1) == code)
        msg[k] = dot(big, cache[...].reshape(512, 1152)).astype(BF).reshape(8, 16, 1152)

    build(3)
    pl.semaphore_wait(barrier, NE - 1 + NG - 1)

    loop(0, 5, lambda j: pltpu.make_async_remote_copy(
        msg.at[3, j], far.at[g, pl.ds(pl.multiple_of(16 * j, 16), 16)], e1s, e1r.at[j // 3],
        device_id={"ep": rank(lax.rem(g - xc + 8, 8), lax.rem(z + 2 + j, 8))}, device_id_type=MESH,
    ).start())
    sent.append(lambda: await_bytes(msg.at[3, pl.ds(0, 5)], e1s))
    loop(0, 3, build)

    def move_near(k):
        def one(j):
            to = rank(j, lax.rem(z + k + 7, 8))
            there = pool.at[k, pl.ds(pl.multiple_of(16 * xc, 16), 16)]

            @pl.when(to == me)
            def _():
                pltpu.make_async_copy(msg.at[k, j], there, n1r.at[k]).start()

            @pl.when(to != me)
            def _():
                pltpu.make_async_remote_copy(
                    msg.at[k, j], there, n1s.at[k], n1r.at[k], device_id={"ep": to}, device_id_type=MESH
                ).start()

        loop(0, 8, one)

    for h in range(2):
        rows = pl.ds(64 * h, 64)
        q_lat = dot(qn[:, 128 * h : 128 * h + 128], ka[h]).astype(BF)
        a, b = iota((128, 128), 0), iota((128, 128), 1)
        rope = dot(qr[...], hot((b < 64) & (a == b + 64 * h))).astype(BF)
        qe[rows, 0:512] = q_lat
        qe[rows, 512:640] = rope
    qo[...] = dot(qe[...], hot(iota((640, 640), 1) == iota((640, 640), 0) + 64)).astype(BF)

    req = iota((16, 64), 0)
    lens = jnp.zeros((16, 64), jnp.int32)
    for i in range(16):
        lens = jnp.where(req == i, len_ref[i], lens)
    count = jnp.clip(lens - 16 * iota((16, 64), 1), 0, 16)
    table = bt[...]
    addr = iota((16, 192), 1)
    usable = jnp.zeros((16, 192), jnp.int32)
    for p in range(64):
        usable = usable + jnp.where(table[:, p : p + 1] == addr, count[:, p : p + 1], 0)
    lam = iota((128, 16), 0)
    spread = hot((lam % 64) // 4 == iota((128, 16), 1))
    use[...] = dot(spread, usable.astype(F32).astype(BF)).astype(BF)

    pool[7, 0:16] = nl[:, 0:1152]
    pool[7, 16:32] = nl[:, 1152:2304]
    pool[7, 32:128] = jnp.zeros((96, 1152), BF)

    acc_e[...] = jnp.zeros_like(acc_e)
    acc_o[...] = jnp.zeros_like(acc_o)
    m_ref[...] = jnp.full_like(m_ref, NEG)
    l_ref[...] = jnp.zeros_like(l_ref)

    def attend(parts):
        scores = []
        m = m_ref[...]
        m_new = m
        for x, c in parts:
            s_e = jnp.where(c > 0.5, dot_nt(qe[...], x[:, 0:640]) * scale, NEG)
            s_o = jnp.where(c > 1.5, dot_nt(qo[...], x[:, 512:1152]) * scale, NEG)
            m_new = jnp.maximum(m_new, jnp.max(jnp.maximum(s_e, s_o), axis=1, keepdims=True))
            scores.append((s_e, s_o))
        f = jnp.exp(m - m_new)
        l = l_ref[...] * f
        out_e = acc_e[...] * f
        out_o = acc_o[...] * f
        for (x, c), (s_e, s_o) in zip(parts, scores):
            p_e = jnp.where(c > 0.5, jnp.exp(s_e - m_new), 0.0)
            p_o = jnp.where(c > 1.5, jnp.exp(s_o - m_new), 0.0)
            l = l + jnp.sum(p_e + p_o, axis=1, keepdims=True)
            out_e = out_e + dot(p_e.astype(BF), x[:, 0:512])
            out_o = out_o + dot(p_o.astype(BF), x[:, 512:1152])
        m_ref[...] = m_new
        l_ref[...] = l
        acc_e[...] = out_e
        acc_o[...] = out_o

    def far_part(o):
        col = iota((192, 80), 1)
        source = rank(lax.rem(o - xc + 8, 8), lax.rem(z + 14 - col // 16, 8))
        place = hot(iota((192, 80), 0) == 64 + 2 * source + (col // 8) % 2)
        return far[o], dot(use[...], place) - (2 * (iota((128, 80), 1) % 8)).astype(F32)

    def attend_pool(i):
        col = iota((192, 128), 1)
        moved = 64 + 2 * rank(col // 16, lax.rem(z + 9 - i, 8)) + (col // 8) % 2
        place = jnp.where(i < 3, moved, col % 64)
        lam, key = iota((128, 128), 0), iota((128, 128), 1)
        pair = jnp.where(i < 3, key % 8, 2 * (i - 3) + key // 64)
        c = dot(use[...], hot(iota((192, 128), 0) == place)) - (2 * pair).astype(F32)
        fresh = jnp.where(((lam % 64) // 4 == key % 16) & (key < 32), lam % 4 + 1 - 2 * (key // 16), 0)
        attend([(pool[i], jnp.where(i == 7, fresh.astype(F32), c))])

    loop(0, 5, lambda q: attend_pool(7 - q))

    def ring_part(at, ssem, rsem, h):
        up = 1 - 2 * h

        def send(o, way):
            pltpu.make_async_remote_copy(
                at(o, h), at(o, h), ssem, rsem.at[h, o], device_id={"grp": peer(way)}, device_id_type=MESH
            ).start()

        def own():
            send(g, up)
            send(g, -up)

        def forward(t):
            a, b = peer(-up * t), peer(up * t)
            await_bytes(at(a, h), rsem.at[h, a])

            @pl.when(t < 4)
            def _():
                send(a, up)
                await_bytes(at(b, h), rsem.at[h, b])

                @pl.when(t < 3)
                def _():
                    send(b, -up)

        return own, forward

    def far_half(o, h):
        return far.at[o, pl.ds(48 * h, 48 - 16 * h)]

    own_0, forward_0 = ring_part(far_half, a1s, a1r, 0)
    own_1, forward_1 = ring_part(far_half, a1s, a1r, 1)
    await_bytes(far_half(g, 0), e1r.at[0])
    own_0()
    await_bytes(far_half(g, 1), e1r.at[1])
    own_1()
    loop(0, 3, move_near)
    sent.append(lambda: await_bytes(msg.at[0], n1s.at[0]))
    sent.append(lambda: await_bytes(msg.at[1, pl.ds(0, 7)], n1s.at[1]))
    sent.append(lambda: await_bytes(msg.at[2], n1s.at[2]))
    attend([far_part(g)])

    def step_far(t):
        forward_0(t)
        forward_1(t)

        @pl.when(t < 4)
        def _():
            attend([far_part(peer(-t)), far_part(peer(t))])

        @pl.when(t > 1)
        def _():
            k = lax.rem(t + 2, 3)
            await_bytes(pool.at[k], n1r.at[k])
            attend_pool(k)

    loop(1, 5, step_far)
    attend([far_part(peer(4))])
    sent.append(lambda: await_bytes(far.at[pl.ds(0, 7)], a1s))
    total = acc_e[...] + acc_o[...][:, 64:576]
    latent = (total / l_ref[...]).astype(BF)
    heads = [dot(latent[64 * h : 64 * h + 64], va[h]).astype(BF) for h in range(2)]
    term = dot(heads[0], op[0:128]) + dot(heads[1], op[128:256])
    for c in range(8):
        p3s[c] = term[:, 256 * c : 256 * c + 256].astype(BF)

    def exchange(src, dst, ssem, rsem):
        loop(1, NG, lambda k: pltpu.make_async_remote_copy(
            src(peer(k)), dst.at[k - 1], ssem, rsem, device_id={"grp": peer(k)}, device_id_type=MESH
        ).start())

    exchange(lambda c: p3s.at[c], p3r, p3ss, p3rs)
    sent.append(lambda: await_bytes(p3s.at[pl.ds(0, 7)], p3ss))
    ids_v = ids[...]
    expert = iota((64, 64), 0)
    named_t = jnp.zeros((64, 64), F32)
    for k in range(6):
        named_t = named_t + jnp.where(ids_v[k : k + 1, :] == expert, 1.0, 0.0)
    identity = hot(iota((64, 64), 0) == iota((64, 64), 1))
    named_b = dot_nt(identity, named_t.astype(BF)).astype(BF)
    before = dot(hot(iota((64, 64), 1) < iota((64, 64), 0)), named_b).astype(BF)
    widen = hot(iota((64, 512), 1) // 8 == iota((64, 512), 0))
    slot = (iota((64, 512), 1) % 8).astype(F32)
    chosen = (dot(named_b, widen) > 0.5) & (jnp.abs(dot(before, widen) - slot) < 0.5)
    chosen_b = hot(chosen)

    await_bytes(p3r, p3rs)
    cols = pl.ds(pl.multiple_of(g * 256, 256), 256)
    attn = p3s[g].astype(F32)
    for k in range(NG - 1):
        attn = attn + p3r[k].astype(F32)
    state = hid[:, cols].astype(F32) + attn
    st[...] = state
    square = jnp.sum(state * state, axis=1, keepdims=True)
    diagonal = iota((64, 128), 0) == iota((64, 128), 1)
    p4s[...] = jnp.broadcast_to(jnp.sum(jnp.where(diagonal, square, 0.0), axis=0, keepdims=True), (8, 128))
    exchange(lambda c: p4s, p4r, p4ss, p4rs)
    sent.append(lambda: await_bytes(p4r, p4ss))
    await_bytes(p4r, p4rs)
    squares = p4s[...]
    for k in range(NG - 1):
        squares = squares + p4r[k]
    square = jnp.sum(jnp.where(diagonal, squares[0:1], 0.0), axis=1, keepdims=True)
    inverse = lax.rsqrt(square / 2048.0 + 1e-06)
    normed = (state * inverse * gain[:, cols].astype(F32)).astype(BF)

    xs[...] = dot_tn(chosen_b, normed).reshape(64, 8, 256).astype(BF)

    def dispatch(n):
        to = rank(lax.rem(n + xc, 8), lax.rem(z + 2 + n // 8, 8))
        there = gath.at[g, 8 * (n // 8) + xc]
        sem = e2r.at[n // 40]

        @pl.when(to == me)
        def _():
            pltpu.make_async_copy(xs.at[me], there, sem).start()

        @pl.when(to != me)
        def _():
            pltpu.make_async_remote_copy(
                xs.at[to], there, e2s, sem, device_id={"ep": to}, device_id_type=MESH
            ).start()

    loop(0, NE, dispatch)
    lgs[...] = dot_nt(normed, router[:, cols])
    exchange(lambda c: lgs, lgr, lgss, lgrs)
    sent.append(lambda: await_bytes(lgr, lgss))
    sent.append(lambda: await_bytes(xs.at[pl.ds(0, 63)], e2s))
    for copy in w_copies:
        copy.wait()
    acc_g[...] = jnp.zeros_like(acc_g)
    acc_u[...] = jnp.zeros_like(acc_u)

    def half(h):
        return pl.ds(40 * h, 40 - 16 * h)

    def rows_of(h):
        return pl.ds(320 * h, 320 - 128 * h)

    def gath_half(o, h):
        return gath.at[o, half(h)]

    def expert_columns(o, h):
        x = gath[o, half(h)].reshape(320 - 128 * h, 256)
        lanes = pl.ds(pl.multiple_of(o * 256, 256), 256)
        acc_g[rows_of(h), :] += dot_nt(x, wg[:, lanes])
        acc_u[rows_of(h), :] += dot_nt(x, wu[:, lanes])

    def both_sides(t, h):
        loop(0, jnp.where(t < 4, 2, 1), lambda i: expert_columns(peer(t * (2 * i - 1)), h))

    def activate(h):
        gate = acc_g[rows_of(h), :]
        act[rows_of(h), :] = (gate / (1.0 + jnp.exp(-gate)) * acc_u[rows_of(h), :]).astype(BF)

    def pass_on(c, h, way):
        d = (1 - way) // 2
        pltpu.make_async_remote_copy(
            part.at[c, half(h)], rsr.at[d, c, half(h)], rss, rsrs.at[d, h, c],
            device_id={"grp": peer(way)}, device_id_type=MESH,
        ).start()

    def make(h):
        up = 1 - 2 * h

        def one(i):
            near = 4 - (i + 1) // 2
            c = peer(jnp.where(i % 2 == 1, -up * near, up * near))
            lanes = pl.ds(pl.multiple_of(c * 256, 256), 256)
            part[c, half(h)] = dot(act[rows_of(h), :], wd[:, lanes]).reshape(40 - 16 * h, 8, 256).astype(BF)

            @pl.when(i == 0)
            def _():
                pass_on(c, h, up)

            @pl.when(i == 1)
            def _():
                pass_on(c, h, -up)

        loop(0, 8, one)

    def add_on(t, h):
        up = 1 - 2 * h

        def stream(i):
            way = up * (1 - 2 * i)
            c = peer(way * (4 - i - t))
            d = (1 - way) // 2
            await_bytes(rsr.at[d, c, half(h)], rsrs.at[d, h, c])
            part[c, half(h)] = (part[c, half(h)].astype(F32) + rsr[d, c, half(h)].astype(F32)).astype(BF)
            pass_on(c, h, way)

        loop(0, jnp.where(t < 3, 2, 1), stream)

    def own_half(h):
        total_h = part[g, half(h)].astype(F32)
        for d in range(2):
            await_bytes(rsr.at[d, g, half(h)], rsrs.at[d, h, g])
            total_h = total_h + rsr[d, g, half(h)].astype(F32)
        ys[half(h)] = total_h.astype(BF)

    def give_back(n):
        to = rank(lax.rem(n + xc, 8), lax.rem(z + 14 - n // 8, 8))
        here = ys.at[8 * (n // 8) + lax.rem(n + xc, 8)]

        @pl.when(to == me)
        def _():
            pltpu.make_async_copy(here, ret.at[me], e3r).start()

        @pl.when(to != me)
        def _():
            pltpu.make_async_remote_copy(
                here, ret.at[me], e3s, e3r, device_id={"ep": to}, device_id_type=MESH
            ).start()

    own_0, forward_0 = ring_part(gath_half, a2s, a2r, 0)
    own_1, forward_1 = ring_part(gath_half, a2s, a2r, 1)
    await_bytes(gath_half(g, 0), e2r.at[0])
    own_0()
    expert_columns(g, 0)

    await_bytes(gath_half(g, 1), e2r.at[1])
    own_1()
    expert_columns(g, 1)

    def step_expert(t):
        forward_0(t)
        forward_1(t)
        for h in range(2):
            both_sides(t, h)

    loop(1, 4, step_expert)
    forward_0(4)
    expert_columns(peer(4), 0)
    activate(0)
    make(0)
    forward_1(4)
    expert_columns(peer(4), 1)
    sent.append(lambda: await_bytes(gath.at[pl.ds(0, 7)], a2s))
    activate(1)
    make(1)

    def step_sum(t):
        add_on(t, 0)
        add_on(t, 1)

    loop(1, 4, step_sum)
    own_half(0)
    loop(0, 40, give_back)
    own_half(1)
    sent.append(lambda: await_bytes(part.at[pl.ds(0, 7)], rss))
    loop(40, NE, give_back)
    sent.append(lambda: await_bytes(ys.at[pl.ds(0, 63)], e3s))

    await_bytes(lgr, lgrs)
    logits = lgs[...]
    for k in range(NG - 1):
        logits = logits + lgr[k]
    weight = jnp.where(named_b.astype(F32) > 0.5, jax.nn.sigmoid(logits), 0.0)
    weight = weight / jnp.sum(weight, axis=1, keepdims=True)
    w_hi = weight.astype(BF)
    w_lo = (weight - w_hi.astype(F32)).astype(BF)
    mask = chosen_b.astype(F32)
    mix_hi = (dot(w_hi, widen) * mask).astype(BF)
    mix_lo = (dot(w_lo, widen) * mask).astype(BF)
    await_bytes(ret, e3r)
    results = ret[...].reshape(512, 256)
    out[...] = (st[...] + dot(mix_hi, results) + dot(mix_lo, results)).astype(BF)

    for wait in sent:
        wait()


def local(
    hidden_in, query_nope, query_rope, new_latent, latent_cache, key_absorb, value_absorb, output_proj, norm_gain,
    router_proj, expert_ids, expert_gate, expert_up, expert_down, block_table, lengths, subtree_moves,
):
    vmem = pl.BlockSpec(memory_space=pltpu.VMEM)
    anywhere = pl.BlockSpec(memory_space=pl.ANY)
    dma = pltpu.SemaphoreType.DMA
    v = pltpu.VMEM
    return pl.pallas_call(
        kernel,
        out_shape=jax.ShapeDtypeStruct((64, 256), BF),
        in_specs=[pl.BlockSpec(memory_space=pltpu.SMEM)] + [vmem] * 12 + [anywhere] * 4,
        out_specs=vmem,
        scratch_shapes=[
            v((176, 2048), BF),
            v((176, 2048), BF),
            v((176, 2048), BF),
            v((4, 8, 16, 1152), BF),
            v((8, 80, 1152), BF),
            v((8, 128, 1152), BF),
            v((128, 640), BF),
            v((128, 640), BF),
            v((128, 192), BF),
            v((128, 1), F32),
            v((128, 1), F32),
            v((128, 512), F32),
            v((128, 640), F32),
            v((8, 64, 256), BF),
            v((7, 64, 256), BF),
            v((8, 128), F32),
            v((7, 8, 128), F32),
            v((64, 64), F32),
            v((7, 64, 64), F32),
            v((64, 256), F32),
            v((64, 8, 256), BF),
            v((8, 64, 8, 256), BF),
            v((512, 176), F32),
            v((512, 176), F32),
            v((512, 176), BF),
            v((8, 64, 8, 256), BF),
            v((2, 8, 64, 8, 256), BF),
            v((64, 8, 256), BF),
            v((64, 8, 256), BF),
            dma, dma((3,)),
            dma, dma((2,)), dma((3,)), dma((3,)), dma, dma((2, 8)),
            dma, dma, dma, dma, dma, dma,
            dma, dma((2,)), dma, dma((2, 8)),
            dma, dma((2, 2, 8)),
            dma, dma,
        ],
        compiler_params=pltpu.CompilerParams(
            collective_id=0, has_side_effects=True, vmem_limit_bytes=56 * 1024 * 1024
        ),
        name="layer",
    )(
        lengths, hidden_in, query_nope, query_rope, new_latent, key_absorb, value_absorb, output_proj,
        norm_gain.reshape(1, -1), router_proj.T, expert_ids.T, block_table, subtree_moves[0].T,
        latent_cache, expert_gate[0].T, expert_up[0].T, expert_down,
    )


def solution(mesh):
    in_specs = (
        P("ep", None), P("ep", "grp"), P("ep", "grp"), P("ep", None), P("ep", None),
        P("grp", None, None), P("grp", None, None), P("grp", None), P(), P(), P("ep", None),
        P("ep", None, "grp"), P("ep", None, "grp"), P("ep", "grp", None), P("ep", None), P("ep"),
        P("ep", None, None),
    )
    return jax.shard_map(local, mesh=mesh, in_specs=in_specs, out_specs=P("ep", "grp"), check_vma=False)
```

time: 141 us -> 128 us (0.908)
  local copies, waits for them, and re-layouts: 10.1 us -> 2.67 us
  Pallas kernels: 131 us -> 125 us
    unnamed x10 -> x1, local copies, waits for them, and re-layouts: 8.73 us -> 1.38 us
    pallas_call x1, Pallas kernels: 131 us -> 125 us  [local(): pl.pallas_call(kernel, out_shape=jax.ShapeDtypeStruct((64, 256), BF), in_...]
where the time goes in v2:
time: 128 us
  Pallas kernels  125 us (98%)
  local copies, waits for them, and re-layouts  2.67 us (2%)
    pallas_call x1, Pallas kernels, local(): pl.pallas_call(kernel, out_shape=jax.ShapeDtypeStruct((64, 256), BF), in_...  125 us

profile of v2, /device:TPU:1, one launch (start us, length us, event | category | flops | bytes accessed | tf_op | source)
XLA Modules:
  0.0 128.0 jit_solution(4851348206079493449)
XLA Ops:
  0.0 1.3 %reshape.3.gain = bf16[1,2048]{1,0:T(2,128)(2,1)} reshape(bf16[2048]{0:T(1024)(128)(2,1)} %param.25) | data formatting | bytes 8192 | tf_op jit(solution)/shard_map/reshape | solution.py:531
  1.3 125.3 %layer.1 = bf16[64,256]{1,0:T(8,128)(2,1)} custom-call(s32[16]{0:T(128)} %len_ref.1, bf16[64,2048]{1,0:T(8,128)(2,1)} %hid.1, bf16[64,256]{1,0:T(8,128)(2,1)} %qn.1, bf16[64,128]{1,0:T(8,128)(2,1)} %qr.1, bf16[16,2304]{1,0:T(8,128)(2,1)} %nl.1, bf16[2,128,512]{2,1,0:T(8,128)(2,1)} %ka.1, bf16[2,512,128]{2,1,0:T(8,128)(2,1)} %va.1, bf16[256,2048]{1,0:T(8,128)(2,1)} %op.1, ...), custom_call_target="tpu_custom_call" | custom-call | tf_op jit(solution)/shard_map/layer/pallas_call | solution.py:483
  126.6 1.4 %copy.19 = bf16[64,256]{1,0:T(8,128)(2,1)} copy(bf16[64,256]{1,0:T(8,128)(2,1)} %layer.1) | data formatting | bytes 65536

commit v3 on v2

--- a/solution.py
+++ b/solution.py
@@ -38,11 +38,11 @@
 
 
 def kernel(
-    len_ref, hid, qn, qr, nl, ka, va, op, gain, router, ids, bt, mv, cache_hbm, wg_hbm, wu_hbm, wd_hbm,
+    len_ref, qn, qr, ka, gain, ids, bt, mv, hid_hbm, nl_hbm, va_hbm, op_hbm, router_hbm, cache_hbm, wg_hbm, wu_hbm, wd_hbm,
     out,
-    wg, wu, wd, msg, far, pool, qe, qo, use, m_ref, l_ref, acc_e, acc_o, p3s, p3r, p4s, p4r, lgs, lgr, st, xs, gath,
-    acc_g, acc_u, act, part, rsr, ys, ret,
-    cache_sem, w_sem, e1s, e1r, n1s, n1r, a1s, a1r, p3ss, p3rs, p4ss, p4rs, lgss, lgrs, e2s, e2r, a2s, a2r, rss, rsrs, e3s, e3r,
+    hid, nl, va, op, router, wg, wu, wd, msg, far, pool, qe, qo, use, m_ref, l_ref, acc_e, acc_o, p3s, p3r, p4s, p4r, nrm, st, xs, gath, xn, gn,
+    acc_g, acc_u, act, part, rsr, ys, ret, yn, rn, mns, mnr,
+    cache_sem, w_sem, e1s, e1r, n1s, n1r, a1s, a1r, p3ss, p3rs, p4ss, p4rs, nxs, nxr, e2s, e2r, n2s, n2r, a2s, a2r, rss, rsrs, e3s, e3r, n3s, n3r, mxs, mxr,
 ):
     g = lax.axis_index("grp")
     me = lax.axis_index("ep")
@@ -74,6 +74,15 @@
         pltpu.make_async_copy(wu_hbm, wu, w_sem.at[1]),
         pltpu.make_async_copy(wd_hbm.at[0], wd, w_sem.at[2]),
     ]
+    o_copies = [
+        pltpu.make_async_copy(nl_hbm, nl, w_sem.at[3]),
+        pltpu.make_async_copy(va_hbm, va, w_sem.at[4]),
+        pltpu.make_async_copy(op_hbm, op, w_sem.at[5]),
+        pltpu.make_async_copy(hid_hbm, hid, w_sem.at[6]),
+        pltpu.make_async_copy(router_hbm, router, w_sem.at[7]),
+    ]
+    for copy in o_copies:
+        copy.start()
     for copy in w_copies:
         copy.start()
 
@@ -82,13 +91,22 @@
 
     def rank(xc_, z_):
         return (xc_ // 2) * 16 + z_ * 2 + xc_ % 2
+
+    def away(j):
+        return jnp.where(j > 4, 2 + j, jnp.where(j % 2 == 0, 2 + j // 2, 6 - j // 2))
+
+    def ahead(j):
+        return lax.rem(z + away(j), 8)
+
+    def behind(j):
+        return lax.rem(z + 16 - away(j), 8)
 
     await_bytes(cache, cache_sem)
 
     def build(k):
         row = iota((128, 64), 0)
         slot_ = row // 16
-        to_far = jnp.where(slot_ < 5, rank(lax.rem(g - xc + 8, 8), lax.rem(z + 2 + slot_, 8)), -1)
+        to_far = jnp.where(slot_ < 5, rank(lax.rem(g - xc + 8, 8), ahead(slot_)), -1)
         to_near = rank(slot_, lax.rem(z + k + 7, 8))
         sel = hot(iota((128, 64), 1) == jnp.where(k == 3, to_far, to_near))
         picked = dot_nt(sel, mv[...].astype(F32).astype(BF))
@@ -103,7 +121,7 @@
 
     loop(0, 5, lambda j: pltpu.make_async_remote_copy(
         msg.at[3, j], far.at[g, pl.ds(pl.multiple_of(16 * j, 16), 16)], e1s, e1r.at[j // 3],
-        device_id={"ep": rank(lax.rem(g - xc + 8, 8), lax.rem(z + 2 + j, 8))}, device_id_type=MESH,
+        device_id={"ep": rank(lax.rem(g - xc + 8, 8), ahead(j))}, device_id_type=MESH,
     ).start())
     sent.append(lambda: await_bytes(msg.at[3, pl.ds(0, 5)], e1s))
     loop(0, 3, build)
@@ -148,6 +166,8 @@
     spread = hot((lam % 64) // 4 == iota((128, 16), 1))
     use[...] = dot(spread, usable.astype(F32).astype(BF)).astype(BF)
 
+    for copy in o_copies:
+        copy.wait()
     pool[7, 0:16] = nl[:, 0:1152]
     pool[7, 16:32] = nl[:, 1152:2304]
     pool[7, 32:128] = jnp.zeros((96, 1152), BF)
@@ -183,7 +203,7 @@
 
     def far_part(o):
         col = iota((192, 80), 1)
-        source = rank(lax.rem(o - xc + 8, 8), lax.rem(z + 14 - col // 16, 8))
+        source = rank(lax.rem(o - xc + 8, 8), behind(col // 16))
         place = hot(iota((192, 80), 0) == 64 + 2 * source + (col // 8) % 2)
         return far[o], dot(use[...], place) - (2 * (iota((128, 80), 1) % 8)).astype(F32)
 
@@ -261,17 +281,26 @@
     total = acc_e[...] + acc_o[...][:, 64:576]
     latent = (total / l_ref[...]).astype(BF)
     heads = [dot(latent[64 * h : 64 * h + 64], va[h]).astype(BF) for h in range(2)]
-    term = dot(heads[0], op[0:128]) + dot(heads[1], op[128:256])
-    for c in range(8):
-        p3s[c] = term[:, 256 * c : 256 * c + 256].astype(BF)
+    head_out = jnp.concatenate(heads, axis=1)
+
+    def attn_block(k):
+        c = peer(k)
+        p3s[c] = dot(head_out, op[:, pl.ds(pl.multiple_of(c * 256, 256), 256)]).astype(BF)
+
+        @pl.when(k > 0)
+        def _():
+            pltpu.make_async_remote_copy(
+                p3s.at[c], p3r.at[k - 1], p3ss, p3rs, device_id={"grp": c}, device_id_type=MESH
+            ).start()
+
+    loop(0, NG, lambda k: attn_block(NG - 1 - k))
+    sent.append(lambda: await_bytes(p3s.at[pl.ds(0, 7)], p3ss))
 
     def exchange(src, dst, ssem, rsem):
         loop(1, NG, lambda k: pltpu.make_async_remote_copy(
             src(peer(k)), dst.at[k - 1], ssem, rsem, device_id={"grp": peer(k)}, device_id_type=MESH
         ).start())
 
-    exchange(lambda c: p3s.at[c], p3r, p3ss, p3rs)
-    sent.append(lambda: await_bytes(p3s.at[pl.ds(0, 7)], p3ss))
     ids_v = ids[...]
     expert = iota((64, 64), 0)
     named_t = jnp.zeros((64, 64), F32)
@@ -280,10 +309,15 @@
     identity = hot(iota((64, 64), 0) == iota((64, 64), 1))
     named_b = dot_nt(identity, named_t.astype(BF)).astype(BF)
     before = dot(hot(iota((64, 64), 1) < iota((64, 64), 0)), named_b).astype(BF)
-    widen = hot(iota((64, 512), 1) // 8 == iota((64, 512), 0))
-    slot = (iota((64, 512), 1) % 8).astype(F32)
-    chosen = (dot(named_b, widen) > 0.5) & (jnp.abs(dot(before, widen) - slot) < 0.5)
-    chosen_b = hot(chosen)
+    def choose(first, slots):
+        col = iota((64, 8 * slots), 1)
+        n = first + col // 8
+        widen = hot(iota((64, 8 * slots), 0) == rank(n % 8, ahead(n // 8)))
+        at_slot = jnp.abs(dot(before, widen) - (col % 8).astype(F32)) < 0.5
+        return widen, hot((dot(named_b, widen) > 0.5) & at_slot)
+
+    widen_far, chosen_far = choose(0, 40)
+    widen_near, chosen_near = choose(40, 24)
 
     await_bytes(p3r, p3rs)
     cols = pl.ds(pl.multiple_of(g * 256, 256), 256)
@@ -303,49 +337,78 @@
         squares = squares + p4r[k]
     square = jnp.sum(jnp.where(diagonal, squares[0:1], 0.0), axis=1, keepdims=True)
     inverse = lax.rsqrt(square / 2048.0 + 1e-06)
-    normed = (state * inverse * gain[:, cols].astype(F32)).astype(BF)
-
-    xs[...] = dot_tn(chosen_b, normed).reshape(64, 8, 256).astype(BF)
+    gains = gain[...].astype(F32).reshape(16, 128)
+    row = iota((16, 128), 0)
+    gain_cols = jnp.concatenate(
+        [jnp.sum(jnp.where(row == 2 * g + i, gains, 0.0), axis=0, keepdims=True) for i in range(2)], axis=1
+    )
+    normed = (state * inverse * gain_cols).astype(BF)
+
+    nrm[g] = normed
+    loop(1, NG, lambda k: pltpu.make_async_remote_copy(
+        nrm.at[g], nrm.at[g], nxs, nxr, device_id={"grp": peer(k)}, device_id_type=MESH
+    ).start())
+    sent.append(lambda: await_bytes(nrm.at[pl.ds(0, 7)], nxs))
+
+    xs[...] = dot_tn(chosen_far, normed).reshape(40, 8, 256).astype(BF)
 
     def dispatch(n):
-        to = rank(lax.rem(n + xc, 8), lax.rem(z + 2 + n // 8, 8))
-        there = gath.at[g, 8 * (n // 8) + xc]
-        sem = e2r.at[n // 40]
-
-        @pl.when(to == me)
-        def _():
-            pltpu.make_async_copy(xs.at[me], there, sem).start()
-
-        @pl.when(to != me)
-        def _():
-            pltpu.make_async_remote_copy(
-                xs.at[to], there, e2s, sem, device_id={"ep": to}, device_id_type=MESH
-            ).start()
-
-    loop(0, NE, dispatch)
-    lgs[...] = dot_nt(normed, router[:, cols])
-    exchange(lambda c: lgs, lgr, lgss, lgrs)
-    sent.append(lambda: await_bytes(lgr, lgss))
-    sent.append(lambda: await_bytes(xs.at[pl.ds(0, 63)], e2s))
+        xt = lax.rem(n + xc, 8)
+        pltpu.make_async_remote_copy(
+            xs.at[8 * (n // 8) + xt], gath.at[g, 8 * (n // 8) + xc], e2s, e2r.at[n // 24],
+            device_id={"ep": rank(xt, ahead(n // 8))}, device_id_type=MESH,
+        ).start()
+
+    loop(0, 40, dispatch)
+    sent.append(lambda: await_bytes(xs, e2s))
+
+    def dispatch_near():
+        await_bytes(nrm.at[pl.ds(0, 7)], nxr)
+
+        def block(o):
+            xn[:, o] = dot_tn(chosen_near, nrm[o]).reshape(24, 8, 256).astype(BF)
+
+        loop(0, 8, block)
+
+        def one(n):
+            xt = lax.rem(n + xc, 8)
+            to = rank(xt, lax.rem(z + 7 + n // 8, 8))
+            here, there = xn.at[8 * (n // 8) + xt], gn.at[8 * (n // 8) + xc]
+
+            @pl.when(to == me)
+            def _():
+                pltpu.make_async_copy(here, there, n2r).start()
+
+            @pl.when(to != me)
+            def _():
+                pltpu.make_async_remote_copy(
+                    here, there, n2s, n2r, device_id={"ep": to}, device_id_type=MESH
+                ).start()
+
+        loop(0, 24, one)
+        sent.append(lambda: await_bytes(xn.at[pl.ds(0, 23)], n2s))
+
     for copy in w_copies:
         copy.wait()
     acc_g[...] = jnp.zeros_like(acc_g)
     acc_u[...] = jnp.zeros_like(acc_u)
 
     def half(h):
-        return pl.ds(40 * h, 40 - 16 * h)
+        return pl.ds(24 * h, 24 - 8 * h)
 
     def rows_of(h):
-        return pl.ds(320 * h, 320 - 128 * h)
+        return pl.ds((0, 192, 320)[h], (192, 128, 192)[h])
 
     def gath_half(o, h):
         return gath.at[o, half(h)]
 
-    def expert_columns(o, h):
-        x = gath[o, half(h)].reshape(320 - 128 * h, 256)
+    def add_columns(x, o, h):
         lanes = pl.ds(pl.multiple_of(o * 256, 256), 256)
         acc_g[rows_of(h), :] += dot_nt(x, wg[:, lanes])
         acc_u[rows_of(h), :] += dot_nt(x, wu[:, lanes])
+
+    def expert_columns(o, h):
+        add_columns(gath[o, half(h)].reshape(192 - 64 * h, 256), o, h)
 
     def both_sides(t, h):
         loop(0, jnp.where(t < 4, 2, 1), lambda i: expert_columns(peer(t * (2 * i - 1)), h))
@@ -368,7 +431,7 @@
             near = 4 - (i + 1) // 2
             c = peer(jnp.where(i % 2 == 1, -up * near, up * near))
             lanes = pl.ds(pl.multiple_of(c * 256, 256), 256)
-            part[c, half(h)] = dot(act[rows_of(h), :], wd[:, lanes]).reshape(40 - 16 * h, 8, 256).astype(BF)
+            part[c, half(h)] = dot(act[rows_of(h), :], wd[:, lanes]).reshape(24 - 8 * h, 8, 256).astype(BF)
 
             @pl.when(i == 0)
             def _():
@@ -401,27 +464,33 @@
         ys[half(h)] = total_h.astype(BF)
 
     def give_back(n):
-        to = rank(lax.rem(n + xc, 8), lax.rem(z + 14 - n // 8, 8))
-        here = ys.at[8 * (n // 8) + lax.rem(n + xc, 8)]
+        xt = lax.rem(n + xc, 8)
+        pltpu.make_async_remote_copy(
+            ys.at[8 * (n // 8) + xt], ret.at[8 * (n // 8) + xc], e3s, e3r,
+            device_id={"ep": rank(xt, behind(n // 8))}, device_id_type=MESH,
+        ).start()
+
+    def give_back_near(n):
+        xt = lax.rem(n + xc, 8)
+        to = rank(xt, lax.rem(z + 9 - n // 8, 8))
+        here, there = yn.at[8 * (n // 8) + xt], rn.at[8 * (n // 8) + xc]
 
         @pl.when(to == me)
         def _():
-            pltpu.make_async_copy(here, ret.at[me], e3r).start()
+            pltpu.make_async_copy(here, there, n3r).start()
 
         @pl.when(to != me)
         def _():
-            pltpu.make_async_remote_copy(
-                here, ret.at[me], e3s, e3r, device_id={"ep": to}, device_id_type=MESH
-            ).start()
+            pltpu.make_async_remote_copy(here, there, n3s, n3r, device_id={"ep": to}, device_id_type=MESH).start()
 
     own_0, forward_0 = ring_part(gath_half, a2s, a2r, 0)
     own_1, forward_1 = ring_part(gath_half, a2s, a2r, 1)
     await_bytes(gath_half(g, 0), e2r.at[0])
     own_0()
-    expert_columns(g, 0)
-
     await_bytes(gath_half(g, 1), e2r.at[1])
     own_1()
+    dispatch_near()
+    expert_columns(g, 0)
     expert_columns(g, 1)
 
     def step_expert(t):
@@ -434,39 +503,65 @@
     forward_0(4)
     expert_columns(peer(4), 0)
     activate(0)
-    make(0)
     forward_1(4)
     expert_columns(peer(4), 1)
-    sent.append(lambda: await_bytes(gath.at[pl.ds(0, 7)], a2s))
     activate(1)
     make(1)
+    make(0)
+    sent.append(lambda: await_bytes(gath.at[pl.ds(0, 7)], a2s))
+
+    def near_block(c):
+        lanes = pl.ds(pl.multiple_of(c * 256, 256), 256)
+        yn[:, c] = dot(act[rows_of(2), :], wd[:, lanes]).reshape(24, 8, 256).astype(BF)
 
     def step_sum(t):
+        add_on(t, 1)
         add_on(t, 0)
-        add_on(t, 1)
+
+        @pl.when(t == 1)
+        def _():
+            await_bytes(gn, n2r)
+            loop(0, 8, lambda o: add_columns(gn[:, o].reshape(192, 256), o, 2))
+            activate(2)
+            loop(0, 8, near_block)
+            loop(0, 24, give_back_near)
 
     loop(1, 4, step_sum)
+    sent.append(lambda: await_bytes(yn.at[pl.ds(0, 23)], n3s))
+    own_half(1)
+    loop(24, 40, give_back)
     own_half(0)
-    loop(0, 40, give_back)
-    own_half(1)
+    loop(0, 24, give_back)
     sent.append(lambda: await_bytes(part.at[pl.ds(0, 7)], rss))
-    loop(40, NE, give_back)
-    sent.append(lambda: await_bytes(ys.at[pl.ds(0, 63)], e3s))
-
-    await_bytes(lgr, lgrs)
-    logits = lgs[...]
-    for k in range(NG - 1):
-        logits = logits + lgr[k]
+    sent.append(lambda: await_bytes(ys, e3s))
+
+    logits = jnp.zeros((64, 64), F32)
+    for o in range(8):
+        logits = logits + dot_nt(nrm[o], router[:, 256 * o : 256 * o + 256])
     weight = jnp.where(named_b.astype(F32) > 0.5, jax.nn.sigmoid(logits), 0.0)
     weight = weight / jnp.sum(weight, axis=1, keepdims=True)
     w_hi = weight.astype(BF)
     w_lo = (weight - w_hi.astype(F32)).astype(BF)
-    mask = chosen_b.astype(F32)
-    mix_hi = (dot(w_hi, widen) * mask).astype(BF)
-    mix_lo = (dot(w_lo, widen) * mask).astype(BF)
+
+    def mixer(widen, chosen):
+        mask = chosen.astype(F32)
+        return (dot(w_hi, widen) * mask).astype(BF), (dot(w_lo, widen) * mask).astype(BF)
+
+    near_hi, near_lo = mixer(widen_near, chosen_near)
+    far_hi, far_lo = mixer(widen_far, chosen_far)
+    await_bytes(rn, n3r)
+    for c in range(8):
+        results = rn[:, c].reshape(192, 256)
+        mns[c] = (dot(near_hi, results) + dot(near_lo, results)).astype(BF)
+    exchange(lambda c: mns.at[c], mnr, mxs, mxr)
+    sent.append(lambda: await_bytes(mnr, mxs))
     await_bytes(ret, e3r)
-    results = ret[...].reshape(512, 256)
-    out[...] = (st[...] + dot(mix_hi, results) + dot(mix_lo, results)).astype(BF)
+    results = ret[...].reshape(320, 256)
+    total = st[...] + dot(far_hi, results) + dot(far_lo, results) + mns[g].astype(F32)
+    await_bytes(mnr, mxr)
+    for k in range(NG - 1):
+        total = total + mnr[k].astype(F32)
+    out[...] = total.astype(BF)
 
     for wait in sent:
         wait()
@@ -483,9 +578,14 @@
     return pl.pallas_call(
         kernel,
         out_shape=jax.ShapeDtypeStruct((64, 256), BF),
-        in_specs=[pl.BlockSpec(memory_space=pltpu.SMEM)] + [vmem] * 12 + [anywhere] * 4,
+        in_specs=[pl.BlockSpec(memory_space=pltpu.SMEM)] + [vmem] * 7 + [anywhere] * 9,
         out_specs=vmem,
         scratch_shapes=[
+            v((64, 2048), BF),
+            v((16, 2304), BF),
+            v((2, 512, 128), BF),
+            v((256, 2048), BF),
+            v((64, 2048), BF),
             v((176, 2048), BF),
             v((176, 2048), BF),
             v((176, 2048), BF),
@@ -503,32 +603,37 @@
             v((7, 64, 256), BF),
             v((8, 128), F32),
             v((7, 8, 128), F32),
-            v((64, 64), F32),
-            v((7, 64, 64), F32),
+            v((8, 64, 256), BF),
             v((64, 256), F32),
-            v((64, 8, 256), BF),
-            v((8, 64, 8, 256), BF),
+            v((40, 8, 256), BF),
+            v((8, 40, 8, 256), BF),
+            v((24, 8, 8, 256), BF),
+            v((24, 8, 8, 256), BF),
             v((512, 176), F32),
             v((512, 176), F32),
             v((512, 176), BF),
-            v((8, 64, 8, 256), BF),
-            v((2, 8, 64, 8, 256), BF),
-            v((64, 8, 256), BF),
-            v((64, 8, 256), BF),
-            dma, dma((3,)),
+            v((8, 40, 8, 256), BF),
+            v((2, 8, 40, 8, 256), BF),
+            v((40, 8, 256), BF),
+            v((40, 8, 256), BF),
+            v((24, 8, 8, 256), BF),
+            v((24, 8, 8, 256), BF),
+            v((8, 64, 256), BF),
+            v((7, 64, 256), BF),
+            dma, dma((8,)),
             dma, dma((2,)), dma((3,)), dma((3,)), dma, dma((2, 8)),
             dma, dma, dma, dma, dma, dma,
-            dma, dma((2,)), dma, dma((2, 8)),
+            dma, dma((2,)), dma, dma, dma, dma((2, 8)),
             dma, dma((2, 2, 8)),
-            dma, dma,
+            dma, dma, dma, dma, dma, dma,
         ],
         compiler_params=pltpu.CompilerParams(
             collective_id=0, has_side_effects=True, vmem_limit_bytes=56 * 1024 * 1024
         ),
         name="layer",
     )(
-        lengths, hidden_in, query_nope, query_rope, new_latent, key_absorb, value_absorb, output_proj,
-        norm_gain.reshape(1, -1), router_proj.T, expert_ids.T, block_table, subtree_moves[0].T,
+        lengths, query_nope, query_rope, key_absorb, norm_gain, expert_ids.T, block_table, subtree_moves[0].T,
+        hidden_in, new_latent, value_absorb, output_proj, router_proj.T,
         latent_cache, expert_gate[0].T, expert_up[0].T, expert_down,
     )
 

time: 128 us -> 116 us (0.906)
  Pallas kernels: 125 us -> 113 us
  local copies, waits for them, and re-layouts: 2.67 us -> 1.38 us
    pallas_call x1, Pallas kernels: 125 us -> 113 us  [local(): pl.pallas_call(kernel, out_shape=jax.ShapeDtypeStruct((64, 256), BF), in_...]
    reshape x1 -> x0, local copies, waits for them, and re-layouts: 1.29 us -> none  [local(): norm_gain.reshape(1, -1)]
where the time goes in v3:
time: 116 us; the launch traced here: 115 us
  Pallas kernels  113 us (97%)
  local copies, waits for them, and re-layouts  1.38 us (1%)
    pallas_call x1, Pallas kernels, local(): pl.pallas_call(kernel, out_shape=jax.ShapeDtypeStruct((64, 256), BF), in_...  113 us

profile of v3, /device:TPU:1, one launch (start us, length us, event | category | flops | bytes accessed | tf_op | source)
XLA Modules:
  0.0 114.8 jit_solution(5651100130229094383)
XLA Ops:
  0.0 113.4 %layer.1 = bf16[64,256]{1,0:T(8,128)(2,1)} custom-call(s32[16]{0:T(128)} %len_ref.1, bf16[64,256]{1,0:T(8,128)(2,1)} %qn.1, bf16[64,128]{1,0:T(8,128)(2,1)} %qr.1, bf16[2,128,512]{2,1,0:T(8,128)(2,1)} %ka.1, bf16[2048]{0:T(1024)(128)(2,1)} %gain.1, s32[6,64]{1,0:T(8,128)} %bitcast.14, s32[16,64]{1,0:T(8,128)} %bt.1, s32[2,64]{1,0:T(2,128)} %bitcast.15, ...), custom_call_target="tpu_custom_call" | custom-call | tf_op jit(solution)/shard_map/layer/pallas_call | solution.py:578
  113.4 1.4 %copy.19 = bf16[64,256]{1,0:T(8,128)(2,1)} copy(bf16[64,256]{1,0:T(8,128)(2,1)} %layer.1) | data formatting | bytes 65536

commit v4 on v3

--- a/solution.py
+++ b/solution.py
@@ -41,7 +41,7 @@
     len_ref, qn, qr, ka, gain, ids, bt, mv, hid_hbm, nl_hbm, va_hbm, op_hbm, router_hbm, cache_hbm, wg_hbm, wu_hbm, wd_hbm,
     out,
     hid, nl, va, op, router, wg, wu, wd, msg, far, pool, qe, qo, use, m_ref, l_ref, acc_e, acc_o, p3s, p3r, p4s, p4r, nrm, st, xs, gath, xn, gn,
-    acc_g, acc_u, act, part, rsr, ys, ret, yn, rn, mns, mnr,
+    acc_g, acc_u, act, part, rsr, ys, ret, yn, rn, mns, mnr, mix_n, mix_f,
     cache_sem, w_sem, e1s, e1r, n1s, n1r, a1s, a1r, p3ss, p3rs, p4ss, p4rs, nxs, nxr, e2s, e2r, n2s, n2r, a2s, a2r, rss, rsrs, e3s, e3r, n3s, n3r, mxs, mxr,
 ):
     g = lax.axis_index("grp")
@@ -120,7 +120,7 @@
     pl.semaphore_wait(barrier, NE - 1 + NG - 1)
 
     loop(0, 5, lambda j: pltpu.make_async_remote_copy(
-        msg.at[3, j], far.at[g, pl.ds(pl.multiple_of(16 * j, 16), 16)], e1s, e1r.at[j // 3],
+        msg.at[3, j], far.at[g, pl.ds(pl.multiple_of(16 * j, 16), 16)], e1s, e1r.at[j],
         device_id={"ep": rank(lax.rem(g - xc + 8, 8), ahead(j))}, device_id_type=MESH,
     ).start())
     sent.append(lambda: await_bytes(msg.at[3, pl.ds(0, 5)], e1s))
@@ -219,61 +219,67 @@
 
     loop(0, 5, lambda q: attend_pool(7 - q))
 
-    def ring_part(at, ssem, rsem, h):
-        up = 1 - 2 * h
-
-        def send(o, way):
+    PARTS = 5
+
+    def upward(h):
+        return 1 - 2 * (h % 2)
+
+    def ring(at, ssem, rsem):
+        def send(o, h, way):
             pltpu.make_async_remote_copy(
                 at(o, h), at(o, h), ssem, rsem.at[h, o], device_id={"grp": peer(way)}, device_id_type=MESH
             ).start()
 
-        def own():
-            send(g, up)
-            send(g, -up)
-
-        def forward(t):
+        def own(h):
+            send(g, h, 1)
+            send(g, h, -1)
+
+        def forward(t, h):
+            up = upward(h)
             a, b = peer(-up * t), peer(up * t)
             await_bytes(at(a, h), rsem.at[h, a])
 
             @pl.when(t < 4)
             def _():
-                send(a, up)
+                send(a, h, up)
                 await_bytes(at(b, h), rsem.at[h, b])
 
                 @pl.when(t < 3)
                 def _():
-                    send(b, -up)
+                    send(b, h, -up)
 
         return own, forward
 
-    def far_half(o, h):
-        return far.at[o, pl.ds(48 * h, 48 - 16 * h)]
-
-    own_0, forward_0 = ring_part(far_half, a1s, a1r, 0)
-    own_1, forward_1 = ring_part(far_half, a1s, a1r, 1)
-    await_bytes(far_half(g, 0), e1r.at[0])
-    own_0()
-    await_bytes(far_half(g, 1), e1r.at[1])
-    own_1()
+    def far_at(o, h):
+        return far.at[o, pl.ds(pl.multiple_of(16 * h, 16), 16)]
+
+    own_far, forward_far = ring(far_at, a1s, a1r)
+
+    def start_far(h):
+        await_bytes(far_at(g, h), e1r.at[h])
+        own_far(h)
+
+    loop(0, PARTS, start_far)
     loop(0, 3, move_near)
     sent.append(lambda: await_bytes(msg.at[0], n1s.at[0]))
     sent.append(lambda: await_bytes(msg.at[1, pl.ds(0, 7)], n1s.at[1]))
     sent.append(lambda: await_bytes(msg.at[2], n1s.at[2]))
     attend([far_part(g)])
 
+    def near_chunk(k):
+        await_bytes(pool.at[k], n1r.at[k])
+        attend_pool(k)
+
     def step_far(t):
-        forward_0(t)
-        forward_1(t)
+        loop(0, PARTS, lambda h: forward_far(t, h))
 
         @pl.when(t < 4)
         def _():
             attend([far_part(peer(-t)), far_part(peer(t))])
 
-        @pl.when(t > 1)
-        def _():
-            k = lax.rem(t + 2, 3)
-            await_bytes(pool.at[k], n1r.at[k])
-            attend_pool(k)
+        @pl.when(t == 3)
+        def _():
+            loop(0, 3, near_chunk)
 
     loop(1, 5, step_far)
     attend([far_part(peer(4))])
@@ -355,7 +361,7 @@
     def dispatch(n):
         xt = lax.rem(n + xc, 8)
         pltpu.make_async_remote_copy(
-            xs.at[8 * (n // 8) + xt], gath.at[g, 8 * (n // 8) + xc], e2s, e2r.at[n // 24],
+            xs.at[8 * (n // 8) + xt], gath.at[g, 8 * (n // 8) + xc], e2s, e2r.at[n // 8],
             device_id={"ep": rank(xt, ahead(n // 8))}, device_id_type=MESH,
         ).start()
 
@@ -364,104 +370,117 @@
 
     def dispatch_near():
         await_bytes(nrm.at[pl.ds(0, 7)], nxr)
-
-        def block(o):
-            xn[:, o] = dot_tn(chosen_near, nrm[o]).reshape(24, 8, 256).astype(BF)
-
-        loop(0, 8, block)
-
-        def one(n):
-            xt = lax.rem(n + xc, 8)
-            to = rank(xt, lax.rem(z + 7 + n // 8, 8))
-            here, there = xn.at[8 * (n // 8) + xt], gn.at[8 * (n // 8) + xc]
-
-            @pl.when(to == me)
-            def _():
-                pltpu.make_async_copy(here, there, n2r).start()
-
-            @pl.when(to != me)
-            def _():
-                pltpu.make_async_remote_copy(
-                    here, there, n2s, n2r, device_id={"ep": to}, device_id_type=MESH
-                ).start()
-
-        loop(0, 24, one)
+        for j in range(3):
+            _, chosen_j = choose(40 + 8 * j, 8)
+
+            def block(o):
+                xn[8 * j : 8 * j + 8, o] = dot_tn(chosen_j, nrm[o]).reshape(8, 8, 256).astype(BF)
+
+            loop(0, 8, block)
+
+            def one(n):
+                xt = lax.rem(n + xc, 8)
+                to = rank(xt, lax.rem(z + 7 + j, 8))
+                here, there = xn.at[8 * j + xt], gn.at[8 * j + xc]
+
+                @pl.when(to == me)
+                def _():
+                    pltpu.make_async_copy(here, there, n2r).start()
+
+                @pl.when(to != me)
+                def _():
+                    pltpu.make_async_remote_copy(
+                        here, there, n2s, n2r, device_id={"ep": to}, device_id_type=MESH
+                    ).start()
+
+            loop(0, 8, one)
         sent.append(lambda: await_bytes(xn.at[pl.ds(0, 23)], n2s))
+
+    def gates():
+        logits = jnp.zeros((64, 64), F32)
+        for o in range(8):
+            logits = logits + dot_nt(nrm[o], router[:, 256 * o : 256 * o + 256])
+        weight = jnp.where(named_b.astype(F32) > 0.5, jax.nn.sigmoid(logits), 0.0)
+        weight = weight / jnp.sum(weight, axis=1, keepdims=True)
+        w_hi = weight.astype(BF)
+        w_lo = (weight - w_hi.astype(F32)).astype(BF)
+        for mix, widen, chosen in ((mix_n, widen_near, chosen_near), (mix_f, widen_far, chosen_far)):
+            mask = chosen.astype(F32)
+            mix[0] = (dot(w_hi, widen) * mask).astype(BF)
+            mix[1] = (dot(w_lo, widen) * mask).astype(BF)
 
     for copy in w_copies:
         copy.wait()
     acc_g[...] = jnp.zeros_like(acc_g)
     acc_u[...] = jnp.zeros_like(acc_u)
 
-    def half(h):
-        return pl.ds(24 * h, 24 - 8 * h)
-
-    def rows_of(h):
-        return pl.ds((0, 192, 320)[h], (192, 128, 192)[h])
-
-    def gath_half(o, h):
-        return gath.at[o, half(h)]
-
-    def add_columns(x, o, h):
+    def part_of(h):
+        return pl.ds(8 * h, 8)
+
+    def gath_at(o, h):
+        return gath.at[o, part_of(h)]
+
+    far_rows, near_rows = pl.ds(0, 320), pl.ds(320, 192)
+
+    def add_columns(x, o, rows):
         lanes = pl.ds(pl.multiple_of(o * 256, 256), 256)
-        acc_g[rows_of(h), :] += dot_nt(x, wg[:, lanes])
-        acc_u[rows_of(h), :] += dot_nt(x, wu[:, lanes])
-
-    def expert_columns(o, h):
-        add_columns(gath[o, half(h)].reshape(192 - 64 * h, 256), o, h)
-
-    def both_sides(t, h):
-        loop(0, jnp.where(t < 4, 2, 1), lambda i: expert_columns(peer(t * (2 * i - 1)), h))
-
-    def activate(h):
-        gate = acc_g[rows_of(h), :]
-        act[rows_of(h), :] = (gate / (1.0 + jnp.exp(-gate)) * acc_u[rows_of(h), :]).astype(BF)
+        acc_g[rows, :] += dot_nt(x, wg[:, lanes])
+        acc_u[rows, :] += dot_nt(x, wu[:, lanes])
+
+    def expert_columns(o):
+        add_columns(gath[o].reshape(320, 256), o, far_rows)
+
+    def activate(rows):
+        gate = acc_g[rows, :]
+        act[rows, :] = (gate / (1.0 + jnp.exp(-gate)) * acc_u[rows, :]).astype(BF)
 
     def pass_on(c, h, way):
         d = (1 - way) // 2
         pltpu.make_async_remote_copy(
-            part.at[c, half(h)], rsr.at[d, c, half(h)], rss, rsrs.at[d, h, c],
+            part.at[c, part_of(h)], rsr.at[d, c, part_of(h)], rss, rsrs.at[d, h, c],
             device_id={"grp": peer(way)}, device_id_type=MESH,
         ).start()
 
-    def make(h):
-        up = 1 - 2 * h
-
-        def one(i):
-            near = 4 - (i + 1) // 2
-            c = peer(jnp.where(i % 2 == 1, -up * near, up * near))
-            lanes = pl.ds(pl.multiple_of(c * 256, 256), 256)
-            part[c, half(h)] = dot(act[rows_of(h), :], wd[:, lanes]).reshape(24 - 8 * h, 8, 256).astype(BF)
-
-            @pl.when(i == 0)
-            def _():
-                pass_on(c, h, up)
-
-            @pl.when(i == 1)
-            def _():
-                pass_on(c, h, -up)
-
-        loop(0, 8, one)
+    def down_block(i):
+        near = 4 - (i + 1) // 2
+        way = 1 - 2 * ((i + 1) % 2)
+        c = peer(way * near)
+        lanes = pl.ds(pl.multiple_of(c * 256, 256), 256)
+        part[c] = dot(act[far_rows, :], wd[:, lanes]).reshape(40, 8, 256).astype(BF)
+
+        @pl.when(i == 0)
+        def _():
+            loop(0, PARTS, lambda h: pass_on(c, PARTS - 1 - h, upward(h)))
+
+        @pl.when((i == 1) | (i == 2))
+        def _():
+            def one(h):
+                @pl.when(upward(h) != way)
+                def _():
+                    pass_on(c, h, way)
+
+            loop(0, PARTS, lambda h: one(PARTS - 1 - h))
 
     def add_on(t, h):
-        up = 1 - 2 * h
+        up = upward(h)
 
         def stream(i):
             way = up * (1 - 2 * i)
             c = peer(way * (4 - i - t))
             d = (1 - way) // 2
-            await_bytes(rsr.at[d, c, half(h)], rsrs.at[d, h, c])
-            part[c, half(h)] = (part[c, half(h)].astype(F32) + rsr[d, c, half(h)].astype(F32)).astype(BF)
+            await_bytes(rsr.at[d, c, part_of(h)], rsrs.at[d, h, c])
+            part[c, part_of(h)] = (part[c, part_of(h)].astype(F32) + rsr[d, c, part_of(h)].astype(F32)).astype(BF)
             pass_on(c, h, way)
 
         loop(0, jnp.where(t < 3, 2, 1), stream)
 
-    def own_half(h):
-        total_h = part[g, half(h)].astype(F32)
+    def finish(h):
+        total_h = part[g, part_of(h)].astype(F32)
         for d in range(2):
-            await_bytes(rsr.at[d, g, half(h)], rsrs.at[d, h, g])
-            total_h = total_h + rsr[d, g, half(h)].astype(F32)
-        ys[half(h)] = total_h.astype(BF)
+            await_bytes(rsr.at[d, g, part_of(h)], rsrs.at[d, h, g])
+            total_h = total_h + rsr[d, g, part_of(h)].astype(F32)
+        ys[part_of(h)] = total_h.astype(BF)
+        loop(8 * h, 8 * h + 8, give_back)
 
     def give_back(n):
         xt = lax.rem(n + xc, 8)
@@ -483,81 +502,72 @@
         def _():
             pltpu.make_async_remote_copy(here, there, n3s, n3r, device_id={"ep": to}, device_id_type=MESH).start()
 
-    own_0, forward_0 = ring_part(gath_half, a2s, a2r, 0)
-    own_1, forward_1 = ring_part(gath_half, a2s, a2r, 1)
-    await_bytes(gath_half(g, 0), e2r.at[0])
-    own_0()
-    await_bytes(gath_half(g, 1), e2r.at[1])
-    own_1()
+    own_rows, forward_rows = ring(gath_at, a2s, a2r)
+
+    def start_rows(h):
+        await_bytes(gath_at(g, h), e2r.at[h])
+        own_rows(h)
+
+    loop(0, PARTS, start_rows)
     dispatch_near()
-    expert_columns(g, 0)
-    expert_columns(g, 1)
+    expert_columns(g)
 
     def step_expert(t):
-        forward_0(t)
-        forward_1(t)
-        for h in range(2):
-            both_sides(t, h)
-
-    loop(1, 4, step_expert)
-    forward_0(4)
-    expert_columns(peer(4), 0)
-    activate(0)
-    forward_1(4)
-    expert_columns(peer(4), 1)
-    activate(1)
-    make(1)
-    make(0)
+        loop(0, PARTS, lambda h: forward_rows(t, h))
+        loop(0, jnp.where(t < 4, 2, 1), lambda i: expert_columns(peer(t * (2 * i - 1))))
+
+        @pl.when(t == 1)
+        def _():
+            gates()
+
+        @pl.when(t == 3)
+        def _():
+            await_bytes(gn, n2r)
+            loop(0, 8, lambda o: add_columns(gn[:, o].reshape(192, 256), o, near_rows))
+            activate(near_rows)
+
+    loop(1, 5, step_expert)
     sent.append(lambda: await_bytes(gath.at[pl.ds(0, 7)], a2s))
+    activate(far_rows)
+    loop(0, 5, down_block)
 
     def near_block(c):
         lanes = pl.ds(pl.multiple_of(c * 256, 256), 256)
-        yn[:, c] = dot(act[rows_of(2), :], wd[:, lanes]).reshape(24, 8, 256).astype(BF)
+        yn[:, c] = dot(act[near_rows, :], wd[:, lanes]).reshape(24, 8, 256).astype(BF)
+
+    def mix_block(k):
+        c = peer(k)
+        results = rn[:, c].reshape(192, 256)
+        mns[c] = (dot(mix_n[0], results) + dot(mix_n[1], results)).astype(BF)
+
+        @pl.when(k > 0)
+        def _():
+            pltpu.make_async_remote_copy(
+                mns.at[c], mnr.at[k - 1], mxs, mxr, device_id={"grp": c}, device_id_type=MESH
+            ).start()
+
+    loop(0, 8, near_block)
+    loop(0, 24, give_back_near)
 
     def step_sum(t):
-        add_on(t, 1)
-        add_on(t, 0)
+        loop(0, PARTS, lambda h: add_on(t, PARTS - 1 - h))
 
         @pl.when(t == 1)
         def _():
-            await_bytes(gn, n2r)
-            loop(0, 8, lambda o: add_columns(gn[:, o].reshape(192, 256), o, 2))
-            activate(2)
-            loop(0, 8, near_block)
-            loop(0, 24, give_back_near)
+            loop(5, 8, down_block)
 
     loop(1, 4, step_sum)
+    await_bytes(rn, n3r)
+    loop(0, NG, lambda k: mix_block(NG - 1 - k))
+    sent.append(lambda: await_bytes(mnr, mxs))
     sent.append(lambda: await_bytes(yn.at[pl.ds(0, 23)], n3s))
-    own_half(1)
-    loop(24, 40, give_back)
-    own_half(0)
-    loop(0, 24, give_back)
+    loop(0, PARTS, lambda h: finish(PARTS - 1 - h))
     sent.append(lambda: await_bytes(part.at[pl.ds(0, 7)], rss))
     sent.append(lambda: await_bytes(ys, e3s))
 
-    logits = jnp.zeros((64, 64), F32)
-    for o in range(8):
-        logits = logits + dot_nt(nrm[o], router[:, 256 * o : 256 * o + 256])
-    weight = jnp.where(named_b.astype(F32) > 0.5, jax.nn.sigmoid(logits), 0.0)
-    weight = weight / jnp.sum(weight, axis=1, keepdims=True)
-    w_hi = weight.astype(BF)
-    w_lo = (weight - w_hi.astype(F32)).astype(BF)
-
-    def mixer(widen, chosen):
-        mask = chosen.astype(F32)
-        return (dot(w_hi, widen) * mask).astype(BF), (dot(w_lo, widen) * mask).astype(BF)
-
-    near_hi, near_lo = mixer(widen_near, chosen_near)
-    far_hi, far_lo = mixer(widen_far, chosen_far)
-    await_bytes(rn, n3r)
-    for c in range(8):
-        results = rn[:, c].reshape(192, 256)
-        mns[c] = (dot(near_hi, results) + dot(near_lo, results)).astype(BF)
-    exchange(lambda c: mns.at[c], mnr, mxs, mxr)
-    sent.append(lambda: await_bytes(mnr, mxs))
     await_bytes(ret, e3r)
     results = ret[...].reshape(320, 256)
-    total = st[...] + dot(far_hi, results) + dot(far_lo, results) + mns[g].astype(F32)
+    total = st[...] + dot(mix_f[0], results) + dot(mix_f[1], results) + mns[g].astype(F32)
     await_bytes(mnr, mxr)
     for k in range(NG - 1):
         total = total + mnr[k].astype(F32)
@@ -620,11 +630,13 @@
             v((24, 8, 8, 256), BF),
             v((8, 64, 256), BF),
             v((7, 64, 256), BF),
+            v((2, 64, 192), BF),
+            v((2, 64, 320), BF),
             dma, dma((8,)),
-            dma, dma((2,)), dma((3,)), dma((3,)), dma, dma((2, 8)),
+            dma, dma((5,)), dma((3,)), dma((3,)), dma, dma((5, 8)),
             dma, dma, dma, dma, dma, dma,
-            dma, dma((2,)), dma, dma, dma, dma((2, 8)),
-            dma, dma((2, 2, 8)),
+            dma, dma((5,)), dma, dma, dma, dma((5, 8)),
+            dma, dma((2, 5, 8)),
             dma, dma, dma, dma, dma, dma,
         ],
         compiler_params=pltpu.CompilerParams(

time: 116 us -> 113 us (0.974)
  Pallas kernels: 113 us -> 111 us
    pallas_call x1, Pallas kernels: 113 us -> 111 us  [local(): pl.pallas_call(kernel, out_shape=jax.ShapeDtypeStruct((64, 256), BF), in_...]
where the time goes in v4:
time: 113 us
  Pallas kernels  111 us (98%)
  local copies, waits for them, and re-layouts  1.38 us (1%)
    pallas_call x1, Pallas kernels, local(): pl.pallas_call(kernel, out_shape=jax.ShapeDtypeStruct((64, 256), BF), in_...  111 us

profile of v4, /device:TPU:1, one launch (start us, length us, event | category | flops | bytes accessed | tf_op | source)
XLA Modules:
  0.0 112.7 jit_solution(7609680302162350765)
XLA Ops:
  0.0 111.3 %layer.1 = bf16[64,256]{1,0:T(8,128)(2,1)} custom-call(s32[16]{0:T(128)} %len_ref.1, bf16[64,256]{1,0:T(8,128)(2,1)} %qn.1, bf16[64,128]{1,0:T(8,128)(2,1)} %qr.1, bf16[2,128,512]{2,1,0:T(8,128)(2,1)} %ka.1, bf16[2048]{0:T(1024)(128)(2,1)} %gain.1, s32[6,64]{1,0:T(8,128)} %bitcast.14, s32[16,64]{1,0:T(8,128)} %bt.1, s32[2,64]{1,0:T(2,128)} %bitcast.15, ...), custom_call_target="tpu_custom_call" | custom-call | tf_op jit(solution)/shard_map/layer/pallas_call | solution.py:588
  111.3 1.4 %copy.19 = bf16[64,256]{1,0:T(8,128)(2,1)} copy(bf16[64,256]{1,0:T(8,128)(2,1)} %layer.1) | data formatting | bytes 65536

commit v5 on v4

--- a/solution.py
+++ b/solution.py
@@ -51,6 +51,9 @@
 
     def peer(k):
         return lax.rem(g + (k + NG), NG)
+
+    def farthest(i):
+        return jnp.where(i % 2 == 1, 4 - (i + 1) // 2, 4 + i // 2)
 
     def loop(lo, hi, body):
         def step(i, carry):
@@ -299,7 +302,7 @@
                 p3s.at[c], p3r.at[k - 1], p3ss, p3rs, device_id={"grp": c}, device_id_type=MESH
             ).start()
 
-    loop(0, NG, lambda k: attn_block(NG - 1 - k))
+    loop(0, NG, lambda i: attn_block(farthest(i)))
     sent.append(lambda: await_bytes(p3s.at[pl.ds(0, 7)], p3ss))
 
     def exchange(src, dst, ssem, rsem):
@@ -351,8 +354,8 @@
     normed = (state * inverse * gain_cols).astype(BF)
 
     nrm[g] = normed
-    loop(1, NG, lambda k: pltpu.make_async_remote_copy(
-        nrm.at[g], nrm.at[g], nxs, nxr, device_id={"grp": peer(k)}, device_id_type=MESH
+    loop(0, NG - 1, lambda i: pltpu.make_async_remote_copy(
+        nrm.at[g], nrm.at[g], nxs, nxr, device_id={"grp": peer(farthest(i))}, device_id_type=MESH
     ).start())
     sent.append(lambda: await_bytes(nrm.at[pl.ds(0, 7)], nxs))
 
@@ -523,7 +526,9 @@
         @pl.when(t == 3)
         def _():
             await_bytes(gn, n2r)
-            loop(0, 8, lambda o: add_columns(gn[:, o].reshape(192, 256), o, near_rows))
+            x = jnp.concatenate([gn[:, o].reshape(192, 256) for o in range(8)], axis=1)
+            acc_g[near_rows, :] = dot_nt(x, wg[...])
+            acc_u[near_rows, :] = dot_nt(x, wu[...])
             activate(near_rows)
 
     loop(1, 5, step_expert)
@@ -558,7 +563,7 @@
 
     loop(1, 4, step_sum)
     await_bytes(rn, n3r)
-    loop(0, NG, lambda k: mix_block(NG - 1 - k))
+    loop(0, NG, lambda i: mix_block(farthest(i)))
     sent.append(lambda: await_bytes(mnr, mxs))
     sent.append(lambda: await_bytes(yn.at[pl.ds(0, 23)], n3s))
     loop(0, PARTS, lambda h: finish(PARTS - 1 - h))

time: 113 us -> 112 us (level)
  no operation moved by 1% of the time
where the time goes in v5:
time: 112 us
  Pallas kernels  111 us (99%)
  local copies, waits for them, and re-layouts  1.38 us (1%)
    pallas_call x1, Pallas kernels, local(): pl.pallas_call(kernel, out_shape=jax.ShapeDtypeStruct((64, 256), BF), in_...  111 us

profile of v5, /device:TPU:1, one launch (start us, length us, event | category | flops | bytes accessed | tf_op | source)
XLA Modules:
  0.0 111.9 jit_solution(7500545094682313352)
XLA Ops:
  0.0 110.5 %layer.1 = bf16[64,256]{1,0:T(8,128)(2,1)} custom-call(s32[16]{0:T(128)} %len_ref.1, bf16[64,256]{1,0:T(8,128)(2,1)} %qn.1, bf16[64,128]{1,0:T(8,128)(2,1)} %qr.1, bf16[2,128,512]{2,1,0:T(8,128)(2,1)} %ka.1, bf16[2048]{0:T(1024)(128)(2,1)} %gain.1, s32[6,64]{1,0:T(8,128)} %bitcast.14, s32[16,64]{1,0:T(8,128)} %bt.1, s32[2,64]{1,0:T(2,128)} %bitcast.15, ...), custom_call_target="tpu_custom_call" | custom-call | tf_op jit(solution)/shard_map/layer/pallas_call | solution.py:593
  110.5 1.4 %copy.19 = bf16[64,256]{1,0:T(8,128)(2,1)} copy(bf16[64,256]{1,0:T(8,128)(2,1)} %layer.1) | data formatting | bytes 65536
